TPU v7x, 1024 devices: a whole 8x8x8 slice. The times are simulated.
1024 devices in a mesh: seg: 64 (over x, y), sub: 16 (over z, core).
Axes of the slice: x: 8, y: 8, z: 8, core: 2. Of those that a mesh axis runs over, the one named last changes fastest.
Arguments:
- multipoles: float32 [121, 524288], P(None, ('seg', 'sub')), may hold values from -6 to 6
- top_multipoles: float32 [121, 1024], P(None, ('seg', 'sub')), may hold values from -6 to 6
- translators: float32 [16, 121, 121], replicated, may hold values from -0.5 to 0.5
- child_shifts: float32 [8, 121, 121], replicated, may hold values from -0.5 to 0.5
- far_operator: float32 [121, 121], replicated, may hold values from -0.5 to 0.5
- far_weights: float32 [65536, 1024], P(('seg', 'sub')), may hold values from -0.1875 to 0.1875
- cell_codes: int32 [1024, 512], P(('seg', 'sub')), may hold values from 0 to 511, each once within a row
- inner_sources: int32 [1024, 16, 64], P(('seg', 'sub')), may hold values from 0 to 543
- inner_targets: int32 [1024, 16, 64], P(('seg', 'sub')), may hold values from 0 to 511
- pair_sources: int32 [1024, 16, 16, 8], P(('seg', 'sub')), may hold values from 0 to 511
- peer_target_cells: int32 [1024, 16, 16, 8], P(('seg', 'sub')), may hold values from 0 to 511
- pair_counts: int32 [1024, 16, 16], P(('seg', 'sub')), may hold values from 0 to 8, as said below
Outputs:
- local_field: float32 [121, 524288], P(None, ('seg', 'sub'))
Inputs may be any that keep to these rules, and one draw needn't show every extreme that they name: `pair_counts`: for each device and peer the counts over all relative positions sum to at most 64; every device has a peer whose counts sum to exactly 64, each of them 0 or 8; which peer and positions is drawn. `cell_codes`: each device's codes are a permutation of 0 to 511.
All inputs are finite; a program needn't handle non-finite values.
Results may differ from a plain program's by a relative error of at most 0.0003.
Values sent between devices are 32-bit elements; how exact they have to be, the bound alone decides.
No kernel may reach another device: no remote copies, remote signals or barrier semaphores. Data moves between devices by JAX's collectives and lax.ppermute only.
A program may use at most 32 MiB of HBM per device.

v0:
```python
import jax
import jax.numpy as jnp
from jax import lax
from jax.sharding import PartitionSpec as P

ORDER = 10
HALO = 16


UPPER_LEVEL = lax.Precision.HIGHEST


def extended(array, sides, width):
    for axis, dim in sides:
        devices, length = (lax.axis_size(axis), array.shape[dim])
        up = [(i, (i + 1) % devices) for i in range(devices - 1)]
        down = [(j, i) for i, j in up]
        last = lax.slice_in_dim(array, length - width, length, axis=dim)
        leading = lax.slice_in_dim(array, 0, width, axis=dim)
        before = lax.ppermute(last, axis, up)
        after = lax.ppermute(leading, axis, down)
        array = jnp.concatenate([before, array, after], axis=dim)
    return array


def degree_signs(window_width):
    index = jnp.arange(window_width)
    degree = jnp.zeros((window_width,), jnp.int32)
    for level in range(1, ORDER + 1):
        degree = degree + (index >= level * level).astype(jnp.int32)
    return (1 - 2 * (degree % 2)).astype(jnp.float32)


def indicator_columns(indices, count):
    return (indices[..., None] == jnp.arange(count)[None, :]).astype(jnp.float32)


def body(
    multipoles,
    top_multipoles,
    translators,
    child_shifts,
    far_operator,
    far_weights,
    cell_codes,
    inner_sources,
    inner_targets,
    pair_sources,
    peer_target_cells,
    pair_counts,
):
    window_width = multipoles.shape[0]
    cell_total = multipoles.shape[1]
    nparent = far_weights.shape[0]
    partner_devices = pair_sources.shape[1]
    offset_total = pair_sources.shape[2]
    slot_positions = pair_sources.shape[3]
    slot_total = offset_total * slot_positions
    signs = degree_signs(window_width)
    sign_adjusted = translators * signs[None, :, None] * signs[None, None, :]
    summed = jnp.dot(
        lax.all_gather(top_multipoles, ("seg", "sub"), axis=1, tiled=True),
        far_weights.T,
        precision=UPPER_LEVEL,
    )
    parent_local = jnp.dot(far_operator, summed, precision=UPPER_LEVEL)
    by_octant = jnp.dot(
        child_shifts.reshape(8 * window_width, window_width), parent_local, precision=UPPER_LEVEL
    ).reshape(8, window_width, nparent)
    table = by_octant.transpose(1, 2, 0).reshape(window_width, 8 * nparent)
    field = jnp.dot(table, indicator_columns(cell_codes[0], cell_total).T, precision=UPPER_LEVEL)
    window = extended(multipoles, (("seg", 1),), HALO)
    inner_count = inner_sources.shape[2]
    sources = jnp.take(window, inner_sources[0].reshape(-1), axis=1).reshape(
        window_width, offset_total, inner_count
    )
    inner_terms = jnp.einsum("okj,joc->koc", translators, sources, precision=UPPER_LEVEL).reshape(
        window_width, offset_total * inner_count
    )
    field = field + jnp.dot(
        inner_terms,
        indicator_columns(inner_targets[0].reshape(-1), cell_total),
        precision=UPPER_LEVEL,
    )
    resident_cells = pair_sources[0]
    valid_mask = (jnp.arange(slot_positions)[None, None, :] < pair_counts[0][..., None]).astype(
        jnp.float32
    )
    departing_terms = jnp.take(multipoles, resident_cells.reshape(-1), axis=1).reshape(
        window_width, partner_devices, offset_total, slot_positions
    )
    departing_terms = (
        (departing_terms * valid_mask[None])
        .transpose(1, 0, 2, 3)
        .reshape(partner_devices, window_width, slot_total)
    )
    enumerated_target_cells = peer_target_cells[0].reshape(partner_devices, slot_total)
    arrived, arrived_ids = (
        lax.all_to_all(departing_terms, "sub", split_axis=0, concat_axis=0, tiled=True),
        lax.all_to_all(enumerated_target_cells, "sub", split_axis=0, concat_axis=0, tiled=True),
    )
    arrived = arrived.reshape(partner_devices, window_width, offset_total, slot_positions)
    forward = jnp.einsum("ifz,bziw->bfiw", translators, arrived, precision=UPPER_LEVEL).reshape(
        partner_devices, window_width, slot_total
    )
    field = field + jnp.einsum(
        "pks,psn->kn", forward, indicator_columns(arrived_ids, cell_total), precision=UPPER_LEVEL
    )
    local_owned_mask = (
        jnp.take(multipoles, arrived_ids.reshape(-1), axis=1)
        .reshape(window_width, partner_devices, offset_total, slot_positions)
        .transpose(1, 0, 2, 3)
    )
    answer_message = jnp.einsum(
        "ifz,bziw->bfiw", sign_adjusted, local_owned_mask, precision=UPPER_LEVEL
    ).reshape(partner_devices, window_width, slot_total)
    received_back = lax.all_to_all(answer_message, "sub", split_axis=0, concat_axis=0, tiled=True)
    received_back = (
        received_back.reshape(partner_devices, window_width, offset_total, slot_positions)
        * valid_mask[:, None]
    )
    received_back = received_back.reshape(partner_devices, window_width, slot_total)
    field = field + jnp.einsum(
        "pks,psn->kn",
        received_back,
        indicator_columns(resident_cells.reshape(partner_devices, slot_total), cell_total),
        precision=UPPER_LEVEL,
    )
    return field


def solution(mesh):
    in_specs = (
        P(None, ("seg", "sub")),
        P(None, ("seg", "sub")),
        P(),
        P(),
        P(),
        P(("seg", "sub"), None),
        P(("seg", "sub"), None),
        P(("seg", "sub"), None, None),
        P(("seg", "sub"), None, None),
        P(("seg", "sub"), None, None, None),
        P(("seg", "sub"), None, None, None),
        P(("seg", "sub"), None, None),
    )
    out_specs = P(None, ("seg", "sub"))
    return jax.shard_map(body, mesh=mesh, in_specs=in_specs, out_specs=out_specs, check_vma=False)
```

profile of v0, /device:TPU:1, one launch (start us, length us, event | category | flops | bytes accessed | tf_op | source)
XLA Modules:
  0.0 179.8 jit_solution(7145182762835055485)
XLA Ops:
  0.0 1.0 copy.100
  1.0 0.7 copy.101
  1.7 18.2 %all-to-all-start.1 = ((s32[16,1,128]{2,1,0:T(1,128)}), s32[16,1,128]{2,1,0:T(1,128)S(1)}, u32[]{:S(2)}, u32[]{:S(2)}) async-start(s32[16,1,128]{2,1,0:T(1,128)} %copy.101), calls=%async_computation.1 | async-start | bytes 16384 | tf_op jit(solution)/shard_map/all_to_all | solution.py:100
  19.9 1.1 copy.90
  20.9 0.6 fusion.55
  21.6 1.3 collective-permute-start.1
  22.8 4.6 %collective-permute-start = (f32[121,16]{0,1:T(8,128)}, f32[121,16]{0,1:T(8,128)}, u32[]{:S(2)}, u32[]{:S(2)}) collective-permute-start(f32[121,16]{0,1:T(8,128)} %get-tuple-element.6), channel_id=1, source_target_pairs={{0,16},{16,32},{32,48},{48,64},{64,80},{80,96},{96,112},{112,128},... | collective-permute-start | bytes 23240 | tf_op jit(solution)/shard_map/ppermute | solution.py:20
  27.5 0.9 copy.94
  28.4 0.1 reshape_squeeze.11
  28.5 0.1 copy.96
  28.6 5.5 %gather_fusion.1 = f32[2048,121]{1,0:T(8,128)S(1)} fusion(f32[121,512]{0,1:T(8,128)S(1)} %copy.90, s32[2048]{0:T(1024)S(1)} %fusion.29), kind=kCustom, calls=%fused_computation.clone | custom fusion | bytes 1990656 | tf_op jit(solution)/shard_map/jit(_take)/gather | solution.py:89
  34.1 0.1 copy.97
  34.2 72.8 %all-gather = f32[1024,1,121]{2,1,0:T(1,128)S(1)} all-gather(f32[1,1,121]{2,1,0:T(1,128)S(1)} %bitcast.84), channel_id=1, replica_groups=mesh['seg'=64,'sub'=16] {'seg','sub'}, dimensions={0}, use_global_device_ids=true | all-gather | bytes 496100 | tf_op jit(solution)/shard_map/all_gather | solution.py:62
  107.0 0.3 broadcast_select_fusion.1
  107.3 0.0 copy-start.8
  107.3 1.4 multiply_bitcast_fusion
  108.7 0.4 fusion.56
  109.2 0.2 fusion.57
  109.4 0.6 broadcast_bitcast_fusion
  110.1 0.1 copy.89
  110.2 0.7 reshape_squeeze.10
  110.9 4.6 %all-to-all-start = ((f32[16,121,128]{1,2,0:T(8,128)}), f32[16,121,128]{1,2,0:T(8,128)}, u32[]{:S(2)}, u32[]{:S(2)}) async-start(f32[16,121,128]{1,2,0:T(8,128)} %multiply_bitcast_fusion), calls=%async_computation | async-start | bytes 2097152 | tf_op jit(solution)/shard_map/all_to_all | solution.py:99
  115.6 1.4 convolution_bitcast_fusion
  116.9 0.2 multiply_bitcast_fusion.1
  117.1 0.6 fusion.30
  117.7 6.4 %gather_fusion.2 = f32[2048,121]{1,0:T(8,128)S(1)} fusion(f32[121,512]{0,1:T(8,128)S(1)} %copy.90, s32[2048]{0:T(1024)} %fusion.30), kind=kCustom, calls=%fused_computation.1.clone | custom fusion | bytes 1990656 | tf_op jit(solution)/shard_map/jit(_take)/gather | solution.py:110
  124.2 0.7 compare_and_fusion
  124.9 0.3 broadcast_select_fusion
  125.2 3.1 %fusion.10 = f32[16,16,8,121]{3,1,2,0:T(8,128)S(1)} fusion(f32[16,121,121,1]{2,0,1,3:T(8,128)S(1)} %multiply_bitcast_fusion.1, f32[121,16,16,8]{0,3,2,1:T(8,128)S(1)} %bitcast.68), kind=kOutput, calls=%fused_computation.17 | convolution fusion | flops 359817216 | bytes 2919488 | tf_op jit(solution)/shard_map/ifz,bziw->bfiw/dot_general | solution.py:114
  128.3 1.4 copy.106
  129.8 13.8 %all-to-all-done = f32[16,121,128]{1,2,0:T(8,128)} async-done(((f32[16,121,128]{1,2,0:T(8,128)}), f32[16,121,128]{1,2,0:T(8,128)}, u32[]{:S(2)}, u32[]{:S(2)}) %all-to-all-start) | async-done | bytes 991264 | tf_op jit(solution)/shard_map/all_to_all | solution.py:99
  143.6 4.4 %all-to-all-start.2 = ((f32[16,121,128]{2,1,0:T(8,128)}), f32[16,121,128]{2,1,0:T(8,128)}, u32[]{:S(2)}, u32[]{:S(2)}) async-start(f32[16,121,128]{2,1,0:T(8,128)} %copy.106), calls=%async_computation.2 | async-start | bytes 2097152 | tf_op jit(solution)/shard_map/all_to_all | solution.py:117
  148.1 0.1 copy.107
  148.1 0.1 lt.79
  148.2 0.2 reshape.213
  148.5 0.8 fusion.21
  149.3 0.1 copy.108
  149.4 0.1 copy.109
  149.5 0.1 eq.66
  149.5 0.8 pad_maximum_fusion
  150.3 2.8 %gather_fusion = f32[1024,121]{1,0:T(8,128)S(1)} fusion(f32[121,544]{0,1:T(8,128)S(1)} %pad_maximum_fusion, s32[1024]{0:T(1024)S(1)} %broadcast_clamp_fusion), kind=kCustom, calls=%fused_computation.2 | custom fusion | bytes 995328 | tf_op jit(solution)/shard_map/jit(_take)/gather | solution.py:74
  153.1 2.2 %fusion.17 = f32[16,64,121]{2,1,0:T(8,128)S(1)} fusion(f32[16,121,121]{2,0,1:T(8,128)S(1)} %copy-done.1, f32[121,16,64]{0,2,1:T(8,128)S(1)} %bitcast.74, pred[16,64]{1,0:T(8,128)(4,1)S(1)} %compare_and_fusion.2), kind=kOutput, calls=%fused_computation.24 | convolution fusion | flops 180032512 | bytes 1929280 | tf_op jit(solution)/shard_map/okj,joc->koc/dot_general | solution.py:77
  155.4 1.8 %copy.98 = f32[16,121,128]{1,0,2:T(8,128)S(1)} copy(f32[16,121,128]{1,2,0:T(8,128)} %all-to-all-done) | data formatting | bytes 1982464 | tf_op jit(solution)/shard_map/all_to_all | solution.py:99
  157.2 2.5 %fusion.13 = f32[16,16,8,121]{3,1,2,0:T(8,128)S(1)} fusion(f32[16,121,16,8]{1,0,3,2:T(8,128)S(1)} %bitcast.70, f32[16,121,121,1]{2,0,1,3:T(8,128)S(1)} %bitcast.67), kind=kOutput, calls=%fused_computation.20 | convolution fusion | flops 359817216 | bytes 2919488 | tf_op jit(solution)/shard_map/ifz,bziw->bfiw/dot_general | solution.py:103
  159.7 1.9 %fusion.8 = f32[121,512]{1,0:T(8,128)S(1)} fusion(s32[16,128]{1,0:T(8,128)S(1)} %bitcast.80, f32[16,121,128]{1,0,2:T(8,128)S(1)} %bitcast.75), kind=kOutput, calls=%fused_computation.14 | convolution fusion | flops 1523580928 | bytes 1247232 | tf_op jit(solution)/shard_map/pks,psn->kn/dot_general | solution.py:106
  161.6 13.5 %all-to-all-done.2 = f32[16,121,128]{2,1,0:T(8,128)} async-done(((f32[16,121,128]{2,1,0:T(8,128)}), f32[16,121,128]{2,1,0:T(8,128)}, u32[]{:S(2)}, u32[]{:S(2)}) %all-to-all-start.2) | async-done | bytes 991264 | tf_op jit(solution)/shard_map/all_to_all | solution.py:117
  175.1 2.9 %fusion.7 = f32[121,512]{1,0:T(8,128)S(1)} fusion(s32[16,128]{1,0:T(8,128)S(1)} %copy.109, f32[16,121,128]{2,1,0:T(8,128)} %all-to-all-done.2, f32[16,128]{1,0:T(8,128)S(1)} %compare_convert_fusion), kind=kOutput, calls=%fused_computation.13 | convolution fusion | flops 1523828736 | bytes 1255424 | tf_op jit(solution)/shard_map/pks,psn->kn/dot_general | solution.py:123
  178.0 1.7 fusion.9
  (44 shorter events, 0.2 us)
Async XLA Ops:
  0.0 108.7 %copy-start = (f32[64,1024]{1,0:T(8,128)S(1)}, f32[64,1024]{1,0:T(8,128)}, u32[]{:S(2)}) copy-start(f32[64,1024]{1,0:T(8,128)} %param.19) | copy-start | bytes 786436
  0.0 28.5 %copy-start.13 = (s32[1,16,16]{2,1,0:T(8,128)S(1)}, s32[1,16,16]{2,1,0:T(8,128)}, u32[]{:S(2)}) copy-start(s32[1,16,16]{2,1,0:T(8,128)} %param.25) | copy-start | bytes 3076
  1.7 109.2 %all-to-all-start.1 = ((s32[16,1,128]{2,1,0:T(1,128)}), s32[16,1,128]{2,1,0:T(1,128)S(1)}, u32[]{:S(2)}, u32[]{:S(2)}) async-start(s32[16,1,128]{2,1,0:T(1,128)} %copy.101), calls=%async_computation.1 | async-start | bytes 16384 | tf_op jit(solution)/shard_map/all_to_all | solution.py:100
  21.6 128.0 %collective-permute-start.1 = (f32[121,16]{0,1:T(8,128)}, f32[121,16]{0,1:T(8,128)}, u32[]{:S(2)}, u32[]{:S(2)}) collective-permute-start(f32[121,16]{0,1:T(8,128)} %get-tuple-element.7), channel_id=1, source_target_pairs={{16,0},{32,16},{48,32},{64,48},{80,64},{96,80},{112,96},{128,112},... | collective-permute-start | bytes 23240 | tf_op jit(solution)/shard_map/ppermute | solution.py:21
  22.8 126.7 %collective-permute-start = (f32[121,16]{0,1:T(8,128)}, f32[121,16]{0,1:T(8,128)}, u32[]{:S(2)}, u32[]{:S(2)}) collective-permute-start(f32[121,16]{0,1:T(8,128)} %get-tuple-element.6), channel_id=1, source_target_pairs={{0,16},{16,32},{32,48},{48,64},{64,80},{80,96},{96,112},{112,128},... | collective-permute-start | bytes 23240 | tf_op jit(solution)/shard_map/ppermute | solution.py:20
  28.6 5.6 %copy-start.15 = (f32[121,1]{0,1:T(1,128)S(1)}, f32[121,1]{0,1:T(1,128)}, u32[]{:S(2)}) copy-start(f32[121,1]{0,1:T(1,128)} %param.15) | copy-start | bytes 1456
  107.3 1.8 %copy-start.8 = (f32[121,121]{1,0:T(8,128)S(1)}, f32[121,121]{1,0:T(8,128)}, u32[]{:S(2)}) copy-start(f32[121,121]{1,0:T(8,128)} %param.18) | copy-start | bytes 175696
  108.7 1.4 copy-start.3
  109.4 0.8 copy-start.9
  110.9 6.0 %copy-start.1 = (f32[16,121,121]{2,0,1:T(8,128)S(1)}, f32[16,121,121]{2,0,1:T(8,128)}, u32[]{:S(2)}) copy-start(f32[16,121,121]{2,0,1:T(8,128)} %param.16) | copy-start | bytes 2811076
  110.9 6.2 %copy-start.6 = (s32[16,1,128]{2,1,0:T(1,128)}, s32[16,1,128]{2,1,0:T(1,128)S(1)}, u32[]{:S(2)}) copy-start(s32[16,1,128]{2,1,0:T(1,128)S(1)} %all-to-all-done.1) | copy-start | bytes 24580
  110.9 32.7 %all-to-all-start = ((f32[16,121,128]{1,2,0:T(8,128)}), f32[16,121,128]{1,2,0:T(8,128)}, u32[]{:S(2)}, u32[]{:S(2)}) async-start(f32[16,121,128]{1,2,0:T(8,128)} %multiply_bitcast_fusion), calls=%async_computation | async-start | bytes 2097152 | tf_op jit(solution)/shard_map/all_to_all | solution.py:99
  129.7 18.3 %copy-start.11 = (s32[1024,1]{0,1:T(1,128)S(1)}, s32[1024,1]{0,1:T(1,128)}, u32[]{:S(2)}) copy-start(s32[1024,1]{0,1:T(1,128)} %reshape_squeeze.10) | copy-start | bytes 12292
  129.7 18.3 %copy-start.5 = (s32[16,128]{0,1:T(8,128)S(1)}, s32[16,128]{0,1:T(8,128)}, u32[]{:S(2)}) copy-start(s32[16,128]{0,1:T(8,128)} %broadcast_bitcast_fusion) | copy-start | bytes 24580
  129.7 18.5 %copy-start.2 = (f32[968,64]{0,1:T(8,128)S(1)}, f32[968,64]{0,1:T(8,128)}, u32[]{:S(2)}) copy-start(f32[968,64]{0,1:T(8,128)} %convolution_bitcast_fusion) | copy-start | bytes 743428
  129.7 18.7 %copy-start.10 = (s32[1,16,64]{2,1,0:T(8,128)S(1)}, s32[1,16,64]{2,1,0:T(8,128)}, u32[]{:S(2)}) copy-start(s32[1,16,64]{2,1,0:T(8,128)} %param.21) | copy-start | bytes 12292
  129.8 18.7 %copy-start.14 = (s32[1,512]{1,0:T(1,128)S(1)}, s32[1,512]{1,0:T(1,128)}, u32[]{:S(2)}) copy-start(s32[1,512]{1,0:T(1,128)} %param.20) | copy-start | bytes 6148
  143.6 31.6 %all-to-all-start.2 = ((f32[16,121,128]{2,1,0:T(8,128)}), f32[16,121,128]{2,1,0:T(8,128)}, u32[]{:S(2)}, u32[]{:S(2)}) async-start(f32[16,121,128]{2,1,0:T(8,128)} %copy.106), calls=%async_computation.2 | async-start | bytes 2097152 | tf_op jit(solution)/shard_map/all_to_all | solution.py:117
  148.0 1.3 copy-start.4
  148.0 1.4 copy-start.12
  157.2 2.5 %copy-start.7 = (s32[16,1,128]{2,1,0:T(1,128)S(1)}, s32[16,1,128]{2,1,0:T(1,128)}, u32[]{:S(2)}) copy-start(s32[16,1,128]{2,1,0:T(1,128)} %copy-done.6) | copy-start | bytes 24580
where the time goes:
time: 180 us
  blocking collectives  72.8 us (40%)
  starting transfers between devices  33.2 us (18%)
  waiting for transfers between devices  27.3 us (15%)
  local copies, waits for them, and re-layouts  24.6 us (14%)
  matrix products  17.2 us (10%)
  other arithmetic  4.35 us (2%)
    all_gather x1, blocking collectives, body(): lax.all_gather(top_multipoles, ('seg', 'sub'), axis=1, tiled=True)  72.8 us
    all_to_all x1, starting transfers between devices, body(): lax.all_to_all(enumerated_target_cells, 'sub', split_axis=0, concat_axis=...  18.2 us
    all_to_all x1, waiting for transfers between devices, body(): lax.all_to_all(departing_terms, 'sub', split_axis=0, concat_axis=0, tiled...  13.8 us
    all_to_all x1, waiting for transfers between devices, body(): lax.all_to_all(answer_message, 'sub', split_axis=0, concat_axis=0, tiled=...  13.5 us
    gather x1, local copies, waits for them, and re-layouts, body(): jnp.take(multipoles, arrived_ids.reshape(-1), axis=1)  6.44 us
    gather x1, local copies, waits for them, and re-layouts, body(): jnp.take(multipoles, resident_cells.reshape(-1), axis=1)  5.46 us
    all_to_all x1, starting transfers between devices, body(): lax.all_to_all(departing_terms, 'sub', split_axis=0, concat_axis=0, tiled...  4.64 us
    ppermute x1, starting transfers between devices, extended(): before = lax.ppermute(last, axis, up)  4.61 us
  transfers between devices with their start and end apart: 5, of which 2 were waited for; matrix products, arithmetic and copies ran while one was open for 22% of the time, Pallas kernels for 0%

commit v1 on v0

v1 whole, which is shorter than its diff:
```python
import jax
import jax.numpy as jnp
from jax import lax
from jax.experimental import pallas as pl
from jax.experimental.pallas import tpu as pltpu
from jax.sharding import PartitionSpec as P

ORDER = 10
HALO = 16
WIDE = 128
F32 = jnp.float32
BF16 = jnp.bfloat16
NT = (((1,), (1,)), ((), ()))
NN = (((1,), (0,)), ((), ()))


def degree_signs(coefs):
    index = lax.broadcasted_iota(jnp.int32, (1, coefs), 1)
    degree = jnp.zeros((1, coefs), jnp.int32)
    for level in range(1, ORDER + 1):
        degree = degree + (index >= level * level).astype(jnp.int32)
    return (1 - 2 * (degree % 2)).astype(F32)


def two_terms(value):
    high = value.astype(BF16)
    return high, (value - high.astype(F32)).astype(BF16)


def both_terms(value, axis):
    return jnp.concatenate(two_terms(value), axis=axis)


def dot(left, right, dims):
    return lax.dot_general(left, right, dims, preferred_element_type=F32)


def dot_exact(left, right, dims):
    return lax.dot_general(
        left, right, dims, precision=lax.Precision.HIGHEST, preferred_element_type=F32
    )


def halves(value):
    return value[:, :WIDE] + value[:, WIDE:]


def as_columns(row):
    return jnp.transpose(jnp.broadcast_to(row, (WIDE, row.shape[1])))


def source_indicator(row, cells):
    columns = as_columns(row)
    parts = []
    for at in range(0, cells, WIDE):
        lane = lax.broadcasted_iota(jnp.int32, columns.shape, 1).astype(F32) + float(at)
        parts.append(jnp.where(columns == lane, 1.0, 0.0).astype(BF16))
    return jnp.concatenate(parts, axis=1)


def target_indicator(row, cells):
    shape = (cells, row.shape[1])
    cell = lax.broadcasted_iota(jnp.int32, shape, 0).astype(F32)
    return jnp.where(jnp.broadcast_to(row, shape) == cell, 1.0, 0.0).astype(BF16)


def translate(columns, operator):
    high, low = two_terms(columns)
    op_high, op_low = two_terms(operator)
    return (
        dot(high, op_high, NT) + dot(low, op_high, NT) + dot(high, op_low, NT)
    )


def inner_kernel(window_ref, source_ref, target_ref, operator_ref, out_ref, moved, total):
    offsets = operator_ref.shape[0]
    cells = out_ref.shape[0]
    span = window_ref.shape[1]
    slots = source_ref.shape[1]
    rows = source_ref.shape[0]
    each = rows * slots // offsets
    window = both_terms(window_ref[...], 0)
    for r in range(rows):
        picked = dot(source_indicator(source_ref[r : r + 1, :], span), window, NT)
        moved[r * slots : (r + 1) * slots, :] = halves(picked)
    total[...] = jnp.zeros_like(total)
    for r in range(rows):
        terms = []
        for o in range(r * slots // each, (r + 1) * slots // each):
            terms.append(translate(moved[o * each : (o + 1) * each, :], operator_ref[o]))
        terms = jnp.concatenate(terms, axis=0)
        total[...] += dot(target_indicator(target_ref[r : r + 1, :], cells), both_terms(terms, 1), NN)
    out_ref[...] = halves(total[...])


def far_kernel(top_ref, weight_ref, far_ref, shift_ref, place_ref, near_ref, out_ref):
    top = jnp.concatenate([top_ref[0][:, None], top_ref[1][:, None]], axis=1)
    top = top.reshape(-1, WIDE)
    summed = dot_exact(weight_ref[...], top, NN)
    parent = dot_exact(summed, far_ref[...], NT)
    table = jnp.concatenate(
        [dot_exact(parent, shift_ref[o], NT) for o in range(shift_ref.shape[0])], axis=0
    )
    table = both_terms(table, 1)
    cells = near_ref.shape[0]
    slots = 128
    for at in range(0, cells, slots):
        picked = dot(source_indicator(place_ref[:, at : at + slots], table.shape[0]), table, NN)
        out_ref[at : at + slots, :] = near_ref[at : at + slots, :] + halves(picked)


def pair_kernel(cells_ref, source_ref, target_ref, operator_ref, near_ref, out_ref, block, moved, total):
    peer = pl.program_id(0)
    coefs, cells = out_ref.shape
    offsets = operator_ref.shape[0]
    sign = degree_signs(WIDE)

    @pl.when(peer == 0)
    def _():
        block[...] = jnp.zeros_like(block)

    block[:coefs, :] = cells_ref[0]
    held = both_terms(block[...], 0)
    for way in range(2):
        picked = halves(dot(source_indicator(source_ref[0, way : way + 1, :], cells), held, NT))
        if way == 1:
            picked = picked * sign
        moved[:, way, peer] = picked.reshape(offsets, -1, WIDE)

    @pl.when(peer == pl.num_programs(0) - 1)
    def _():
        total[...] = jnp.zeros_like(total)
        for o in range(offsets):
            terms = translate(moved[o].reshape(-1, WIDE), operator_ref[o])
            count = terms.shape[0] // 2
            terms = jnp.concatenate([terms[:count], terms[count:] * sign], axis=0)
            total[...] += dot(target_indicator(target_ref[o : o + 1, :], cells), both_terms(terms, 1), NN)
        result = near_ref[...] + halves(total[...])
        out_ref[...] = jnp.transpose(result)[:coefs, :]


def whole(shape):
    return pl.BlockSpec(shape, lambda *_: (0,) * len(shape))


def body(
    multipoles,
    top_multipoles,
    translators,
    child_shifts,
    far_operator,
    far_weights,
    cell_codes,
    inner_sources,
    inner_targets,
    pair_sources,
    peer_target_cells,
    pair_counts,
):
    coefs, cells = multipoles.shape
    parents = far_weights.shape[0]
    peers, offsets, room = pair_sources.shape[1:]
    slots = offsets * room
    pad = WIDE - coefs
    segs = lax.axis_size("seg")
    params = pltpu.CompilerParams(vmem_limit_bytes=48 * 1024 * 1024)

    group = lax.all_gather(multipoles, "sub", axis=0, tiled=False)

    used = lax.broadcasted_iota(jnp.int32, (peers, offsets, room), 2) < pair_counts[0][..., None]
    own_source = jnp.where(used, pair_sources[0], -1).reshape(peers, slots).astype(F32)
    own_target = jnp.where(used, peer_target_cells[0], -1).reshape(peers, slots).astype(F32)
    top = jnp.broadcast_to(jnp.pad(top_multipoles[:, 0], (0, pad))[None], (peers, WIDE))
    message = jnp.stack([own_source, own_target, top], axis=1)
    arrived = lax.all_to_all(message, "sub", split_axis=0, concat_axis=0, tiled=True)
    their_source, their_target, tops = arrived[:, 0], arrived[:, 1], arrived[:, 2]

    core = lax.axis_index("sub") % 2
    half = peers // 2
    mine = lax.dynamic_slice_in_dim(tops, core * half, half, axis=0)
    spread = lax.all_to_all(
        jnp.broadcast_to(mine[None], (segs, half, WIDE)), "seg", split_axis=0, concat_axis=0, tiled=True
    )
    every_top = lax.all_gather(
        spread,
        "sub",
        axis=0,
        tiled=False,
        axis_index_groups=[[2 * i, 2 * i + 1] for i in range(half)],
    )

    up = [(i, i + 1) for i in range(segs - 1)]
    down = [(j, i) for i, j in up]
    before = lax.ppermute(multipoles[:, cells - HALO :], "seg", up)
    after = lax.ppermute(multipoles[:, :HALO], "seg", down)
    window = jnp.concatenate([before, multipoles, after], axis=1)
    span = cells + WIDE
    window = jnp.pad(window, ((0, pad), (0, span - window.shape[1])))

    operators = jnp.pad(translators, ((0, 0), (0, pad), (0, pad)))
    shifts = jnp.pad(child_shifts, ((0, 0), (0, pad), (0, pad)))
    far = jnp.pad(far_operator, ((0, pad), (0, pad)))

    inner_rows = inner_sources.shape[1] * inner_sources.shape[2] // 128
    near = pl.pallas_call(
        inner_kernel,
        out_shape=jax.ShapeDtypeStruct((cells, WIDE), F32),
        scratch_shapes=[
            pltpu.VMEM((inner_rows * 128, WIDE), F32),
            pltpu.VMEM((cells, 2 * WIDE), F32),
        ],
        compiler_params=params,
        cost_estimate=pl.CostEstimate(flops=2 * 10**9, bytes_accessed=3 * 10**6, transcendentals=0),
        name="inner_pairs",
    )(
        window,
        inner_sources[0].reshape(inner_rows, 128).astype(F32),
        inner_targets[0].reshape(inner_rows, 128).astype(F32),
        operators,
    )

    octants = child_shifts.shape[0]
    place = (cell_codes % octants * parents + cell_codes // octants).astype(F32)
    near = pl.pallas_call(
        far_kernel,
        out_shape=jax.ShapeDtypeStruct((cells, WIDE), F32),
        compiler_params=params,
        cost_estimate=pl.CostEstimate(flops=10**9, bytes_accessed=2 * 10**6, transcendentals=0),
        name="far_field",
    )(every_top, far_weights, far, shifts, place, near)

    sources = jnp.stack([their_source, own_target], axis=1)
    targets = jnp.stack([their_target, own_source], axis=0)
    targets = targets.reshape(2, peers, offsets, room).transpose(2, 0, 1, 3).reshape(offsets, -1)
    return pl.pallas_call(
        pair_kernel,
        grid=(peers,),
        in_specs=[
            pl.BlockSpec((1, coefs, cells), lambda p: (p, 0, 0)),
            pl.BlockSpec((1, 2, slots), lambda p: (p, 0, 0)),
            whole(targets.shape),
            whole(operators.shape),
            whole(near.shape),
        ],
        out_specs=whole((coefs, cells)),
        out_shape=jax.ShapeDtypeStruct((coefs, cells), F32),
        scratch_shapes=[
            pltpu.VMEM((WIDE, cells), F32),
            pltpu.VMEM((offsets, 2, peers, room, WIDE), F32),
            pltpu.VMEM((cells, 2 * WIDE), F32),
        ],
        compiler_params=params,
        cost_estimate=pl.CostEstimate(flops=6 * 10**9, bytes_accessed=6 * 10**6, transcendentals=0),
        name="pair_terms",
    )(group, sources, targets, operators, near)


def solution(mesh):
    in_specs = (
        P(None, ("seg", "sub")),
        P(None, ("seg", "sub")),
        P(),
        P(),
        P(),
        P(("seg", "sub"), None),
        P(("seg", "sub"), None),
        P(("seg", "sub"), None, None),
        P(("seg", "sub"), None, None),
        P(("seg", "sub"), None, None, None),
        P(("seg", "sub"), None, None, None),
        P(("seg", "sub"), None, None),
    )
    out_specs = P(None, ("seg", "sub"))
    return jax.shard_map(body, mesh=mesh, in_specs=in_specs, out_specs=out_specs, check_vma=False)
```

time: 180 us -> 92.8 us (0.52)
  blocking collectives: 72.8 us -> 4.9 us
  waiting for transfers between devices: 27.3 us -> 9.77 us
  matrix products: 17.2 us -> 0 us
  local copies, waits for them, and re-layouts: 24.6 us -> 9.73 us
  Pallas kernels: 0 us -> 14.7 us
  between operations: 0.38 us -> 13.6 us
  starting transfers between devices: 33.2 us -> 38 us
  other arithmetic: 4.35 us -> 1.59 us
    all_gather x1, blocking collectives: 72.8 us -> 4.9 us  [body(): lax.all_gather(spread, 'sub', axis=0, tiled=False, axis_index_groups=[[2...]
    all_to_all x3 -> x2, waiting for transfers between devices: 27.3 us -> 9.06 us  [the longest x1 9.06 us: body(): lax.all_to_all(jnp.broadcast_to(mine[None], (segs, half, WIDE)), 'seg', s...]
    dot_general x10 -> x0, matrix products: 17.2 us -> none  [the longest x1 3.08 us: body(): jnp.einsum('ifz,bziw->bfiw', sign_adjusted, local_owned_mask, precision=U...]
    gather x3 -> x0, local copies, waits for them, and re-layouts: 14.7 us -> none  [the longest x1 6.44 us: body(): jnp.take(multipoles, arrived_ids.reshape(-1), axis=1)]
    pallas_call x0 -> x3, Pallas kernels: none -> 14.7 us  [the longest x1 9.44 us: body(): pl.pallas_call(pair_kernel, grid=(peers,), in_specs=[pl.BlockSpec((1, coe...]
    all_to_all x3 -> x2, starting transfers between devices: 27.3 us -> 33.3 us  [the longest x1 18.2 us: body(): lax.all_to_all(message, 'sub', split_axis=0, concat_axis=0, tiled=True)]
    unnamed x37 -> x18, local copies, waits for them, and re-layouts: 3.26 us -> 5.77 us
    all_to_all x2 -> x0, local copies, waits for them, and re-layouts: 2.51 us -> none  [the longest x1 1.84 us: body(): lax.all_to_all(departing_terms, 'sub', split_axis=0, concat_axis=0, tiled...]
  transfers between devices with their start and end apart: 5 -> 5, of which waited for: 2 -> 1; matrix products, arithmetic and copies ran while one was open for 22% -> 10% of each run, Pallas kernels for 0% -> 6%
where the time goes in v1:
time: 92.8 us; the launch traced here: 92.3 us
  starting transfers between devices  38 us (41%)
  Pallas kernels  14.7 us (16%)
  between operations  13.6 us (15%)
  waiting for transfers between devices  9.77 us (11%)
  local copies, waits for them, and re-layouts  9.73 us (10%)
  blocking collectives  4.9 us (5%)
  other arithmetic  1.59 us (2%)
    all_to_all x1, starting transfers between devices, body(): lax.all_to_all(message, 'sub', split_axis=0, concat_axis=0, tiled=True)  18.2 us
    all_to_all x1, starting transfers between devices, body(): lax.all_to_all(jnp.broadcast_to(mine[None], (segs, half, WIDE)), 'seg', s...  15.1 us
    pallas_call x1, Pallas kernels, body(): pl.pallas_call(pair_kernel, grid=(peers,), in_specs=[pl.BlockSpec((1, coe...  9.44 us
    all_to_all x1, waiting for transfers between devices, body(): lax.all_to_all(jnp.broadcast_to(mine[None], (segs, half, WIDE)), 'seg', s...  9.06 us
    unnamed x18, local copies, waits for them, and re-layouts  5.77 us
    all_gather x1, blocking collectives, body(): lax.all_gather(spread, 'sub', axis=0, tiled=False, axis_index_groups=[[2...  4.9 us
    ppermute x1, starting transfers between devices, body(): before = lax.ppermute(multipoles[:, cells - HALO:], 'seg', up)  3.34 us
    pallas_call x1, Pallas kernels, body(): pl.pallas_call(inner_kernel, out_shape=jax.ShapeDtypeStruct((cells, WIDE)...  3.18 us
  transfers between devices with their start and end apart: 5, of which 1 were waited for; matrix products, arithmetic and copies ran while one was open for 10% of the time, Pallas kernels for 6%

profile of v1, /device:TPU:1, one launch (start us, length us, event | category | flops | bytes accessed | tf_op | source)
XLA Modules:
  0.0 92.3 jit_solution(10020603904300826873)
XLA Ops:
  6.5 0.0 copy-start.5
  6.5 0.0 copy-start.6
  6.5 0.0 copy-start.3
  6.5 0.0 all-gather.5.cloned.1.call-start
  6.6 0.7 all-gather.5.cloned.1.call-update
  7.3 0.8 copy.32
  8.1 0.1 copy.33
  8.1 1.0 %copy.34 = s32[1,16,16,8]{1,3,2,0:T(8,128)S(1)} copy(s32[1,16,16,8]{2,3,1,0:T(8,128)} %param.21) | data formatting | bytes 16384 | tf_op args[9]
  9.1 0.1 copy.35
  9.1 1.0 %copy.36 = s32[1,16,16,8]{1,3,2,0:T(8,128)S(1)} copy(s32[1,16,16,8]{2,3,1,0:T(8,128)} %param.22) | data formatting | bytes 16384 | tf_op args[10]
  10.1 0.1 copy.37
  10.1 0.1 iota.18
  10.3 0.7 pad.20
  11.0 0.6 pad_maximum_fusion
  11.6 18.2 %all-to-all-start = ((f32[16,3,128]{2,1,0:T(4,128)}), f32[16,3,128]{2,1,0:T(4,128)S(1)}, u32[]{:S(2)}, u32[]{:S(2)}) async-start(f32[16,3,128]{2,1,0:T(4,128)} %pad_maximum_fusion), calls=%async_computation | async-start | bytes 65536 | tf_op jit(solution)/shard_map/all_to_all | solution.py:175
  29.8 1.0 %fusion.5 = (f32[121,16]{1,0:T(8,128)S(1)}, f32[121,16]{1,0:T(8,128)S(1)}) fusion(f32[121,512]{1,0:T(8,128)} %param.12), kind=kLoop, calls=%fused_computation.23 | loop fusion | bytes 30976 | tf_op jit(solution)/shard_map/slice | solution.py:194
  30.7 3.3 %collective-permute-start = (f32[121,16]{1,0:T(8,128)S(1)}, f32[121,16]{1,0:T(8,128)S(1)}, u32[]{:S(2)}, u32[]{:S(2)}) collective-permute-start(f32[121,16]{1,0:T(8,128)S(1)} %get-tuple-element.5), channel_id=1, source_target_pairs={{0,16},{16,32},{32,48},{48,64},{64,80},{80,96},{96,112},{112,128},... | collective-permute-start | bytes 23240 | tf_op jit(solution)/shard_map/ppermute | solution.py:194
  34.1 1.3 %collective-permute-start.1 = (f32[121,16]{1,0:T(8,128)S(1)}, f32[121,16]{1,0:T(8,128)S(1)}, u32[]{:S(2)}, u32[]{:S(2)}) collective-permute-start(f32[121,16]{1,0:T(8,128)S(1)} %get-tuple-element.6), channel_id=1, source_target_pairs={{16,0},{32,16},{48,32},{64,48},{80,64},{96,80},{112,96},{128,112},... | collective-permute-start | bytes 23240 | tf_op jit(solution)/shard_map/ppermute | solution.py:195
  35.4 0.7 fusion.4.place_ref
  36.1 1.5 %copy.42 = f32[16,121,121]{2,1,0:T(8,128)S(1)} copy(f32[16,121,121]{2,0,1:T(8,128)} %param.14) | data formatting | bytes 1874048 | tf_op args[2]
  37.7 0.1 pad.21.operator_ref
  37.8 0.0 copy-done.5
  37.8 0.1 convert_element_type.52.source_ref
  37.8 0.0 copy-done.6
  37.9 0.1 convert_element_type.54.target_ref
  37.9 0.0 copy-done.3
  37.9 0.1 copy.43
  38.1 0.0 copy-done.4
  38.1 0.0 all-to-all-done
  38.2 0.7 broadcast_in_dim.19
  38.9 15.1 %all-to-all-start.1 = ((f32[64,8,128]{2,1,0:T(8,128)}), f32[64,8,128]{2,1,0:T(8,128)S(1)}, u32[]{:S(2)}, u32[]{:S(2)}) async-start(f32[64,8,128]{2,1,0:T(8,128)} %broadcast_in_dim.19), calls=%async_computation.1 | async-start | bytes 524288 | tf_op jit(solution)/shard_map/all_to_all | solution.py:181
  54.0 0.0 collective-permute-done
  54.0 0.0 collective-permute-done.1
  54.0 0.0 copy-done.2
  54.0 0.2 select_maximum_fusion.window_ref
  54.2 0.0 copy-start.1
  54.2 3.2 %inner_pairs.1.near_ref = f32[512,128]{1,0:T(8,128)S(1)} custom-call(f32[128,640]{1,0:T(8,128)S(1)} %select_maximum_fusion.window_ref, f32[8,128]{1,0:T(8,128)S(1)} %convert_element_type.52.source_ref, f32[8,128]{1,0:T(8,128)S(1)} %convert_element_type.54.target_ref, f32[16,128,128]{2,1,0:T(8,128)S(1)} %pad.21.operator_ref), custom_call_target="tpu_custom_call" | custom-call | flops 2000000000 | bytes 3000000 | tf_op jit(solution)/shard_map/inner_pairs/pallas_call | solution.py:205
  57.4 0.1 copy.38
  57.5 0.1 copy.41
  57.7 0.1 copy.44.target_ref
  57.8 9.1 %all-to-all-done.1 = f32[64,8,128]{2,1,0:T(8,128)S(1)} async-done(((f32[64,8,128]{2,1,0:T(8,128)}), f32[64,8,128]{2,1,0:T(8,128)S(1)}, u32[]{:S(2)}, u32[]{:S(2)}) %all-to-all-start.1) | async-done | bytes 262176 | tf_op jit(solution)/shard_map/all_to_all | solution.py:181
  66.8 4.9 %all-gather.1 = f32[128,8,128]{2,1,0:T(8,128)S(1)} all-gather(f32[64,8,128]{2,1,0:T(8,128)S(1)} %all-to-all-done.1), channel_id=3, replica_groups={{0,1},{2,3},{4,5},{6,7},{8,9},{10,11},{12,13},{14,15},{16,17},{18,19},{..., dimensions={0}, use_global_device_ids=true | all-gather | bytes 786432 | tf_op jit(solution)/shard_map/all_gather | solution.py:184
  71.7 0.0 copy-done.1
  71.7 2.0 %far_field.1.near_ref = f32[512,128]{1,0:T(8,128)S(1)} custom-call(f32[2,64,8,128]{3,2,1,0:T(8,128)S(1)} %bitcast.13, f32[64,1024]{1,0:T(8,128)S(1)} %copy-done.1, f32[128,128]{1,0:T(8,128)S(1)} %pad.22.far_ref, f32[8,128,128]{2,1,0:T(8,128)S(1)} %pad.23.shift_ref, f32[1,512]{1,0:T(1,128)S(1)} %fusion.4.place_ref, f32[512,128]{1,0:T(8,128)S(1)} %inner_pairs.1.near_ref), custom_call_target="tpu_custom_call" | custom-call | flops 1000000000 | bytes 2000000 | tf_op jit(solution)/shard_map/far_field/pallas_call | solution.py:224
  73.8 0.0 all-gather.5.cloned.1.call-done.cells_ref
  73.8 0.0 copy-start
  73.8 2.2 %copy-done = f32[16,121,512]{2,1,0:T(8,128)S(1)} copy-done((f32[16,121,512]{2,1,0:T(8,128)S(1)}, f32[16,121,512]{2,1,0:T(8,128)}, u32[]{:S(2)}) %copy-start) | copy-done | bytes 3964952
  76.0 9.4 %pair_terms.1 = f32[121,512]{1,0:T(8,128)} custom-call(f32[16,121,512]{2,1,0:T(8,128)S(1)} %copy-done, f32[16,2,128]{2,1,0:T(2,128)S(1)} %pad_maximum_fusion.1.source_ref, f32[16,256]{1,0:T(8,128)S(1)} %copy.44.target_ref, f32[16,128,128]{2,1,0:T(8,128)S(1)} %pad.21.operator_ref, f32[512,128]{1,0:T(8,128)S(1)} %far_field.1.near_ref), custom_call_target="tpu_custom_call" | custom-call | flops 6000000000 | bytes 6000000 | tf_op jit(solution)/shard_map/pair_terms/pallas_call | solution.py:235
  (15 shorter events, 0.2 us)
Async XLA Ops:
  6.5 31.2 %copy-start.5 = (s32[1,16,64]{2,1,0:T(8,128)S(1)}, s32[1,16,64]{2,1,0:T(8,128)}, u32[]{:S(2)}) copy-start(s32[1,16,64]{2,1,0:T(8,128)} %param.19) | copy-start | bytes 12292
  6.5 31.3 %copy-start.6 = (s32[1,16,64]{2,1,0:T(8,128)S(1)}, s32[1,16,64]{2,1,0:T(8,128)}, u32[]{:S(2)}) copy-start(s32[1,16,64]{2,1,0:T(8,128)} %param.20) | copy-start | bytes 12292
  6.5 31.4 %copy-start.3 = (f32[8,121,121]{2,0,1:T(8,128)S(1)}, f32[8,121,121]{2,0,1:T(8,128)}, u32[]{:S(2)}) copy-start(f32[8,121,121]{2,0,1:T(8,128)} %param.15) | copy-start | bytes 1405540
  6.5 31.5 %copy-start.4 = (f32[121,121]{1,0:T(8,128)S(1)}, f32[121,121]{1,0:T(8,128)}, u32[]{:S(2)}) copy-start(f32[121,121]{1,0:T(8,128)} %param.16) | copy-start | bytes 175696
  6.5 67.2 %all-gather.5.cloned.1.call-start = ((), (), s32[]{:S(2)}) async-start(), calls=%async_computation.2 | async-start | bytes 4456448 | tf_op jit(solution)/shard_map/all_gather | solution.py:168
  8.0 46.0 %copy-start.2 = (f32[121,512]{1,0:T(8,128)S(1)}, f32[121,512]{1,0:T(8,128)}, u32[]{:S(2)}) copy-start(f32[121,512]{1,0:T(8,128)} %param.12) | copy-start | bytes 743428
  11.6 26.5 %all-to-all-start = ((f32[16,3,128]{2,1,0:T(4,128)}), f32[16,3,128]{2,1,0:T(4,128)S(1)}, u32[]{:S(2)}, u32[]{:S(2)}) async-start(f32[16,3,128]{2,1,0:T(4,128)} %pad_maximum_fusion), calls=%async_computation | async-start | bytes 65536 | tf_op jit(solution)/shard_map/all_to_all | solution.py:175
  30.7 23.3 %collective-permute-start = (f32[121,16]{1,0:T(8,128)S(1)}, f32[121,16]{1,0:T(8,128)S(1)}, u32[]{:S(2)}, u32[]{:S(2)}) collective-permute-start(f32[121,16]{1,0:T(8,128)S(1)} %get-tuple-element.5), channel_id=1, source_target_pairs={{0,16},{16,32},{32,48},{48,64},{64,80},{80,96},{96,112},{112,128},... | collective-permute-start | bytes 23240 | tf_op jit(solution)/shard_map/ppermute | solution.py:194
  34.1 19.9 %collective-permute-start.1 = (f32[121,16]{1,0:T(8,128)S(1)}, f32[121,16]{1,0:T(8,128)S(1)}, u32[]{:S(2)}, u32[]{:S(2)}) collective-permute-start(f32[121,16]{1,0:T(8,128)S(1)} %get-tuple-element.6), channel_id=1, source_target_pairs={{16,0},{32,16},{48,32},{64,48},{80,64},{96,80},{112,96},{128,112},... | collective-permute-start | bytes 23240 | tf_op jit(solution)/shard_map/ppermute | solution.py:195
  38.9 27.9 %all-to-all-start.1 = ((f32[64,8,128]{2,1,0:T(8,128)}), f32[64,8,128]{2,1,0:T(8,128)S(1)}, u32[]{:S(2)}, u32[]{:S(2)}) async-start(f32[64,8,128]{2,1,0:T(8,128)} %broadcast_in_dim.19), calls=%async_computation.1 | async-start | bytes 524288 | tf_op jit(solution)/shard_map/all_to_all | solution.py:181
  54.2 17.5 %copy-start.1 = (f32[64,1024]{1,0:T(8,128)S(1)}, f32[64,1024]{1,0:T(8,128)}, u32[]{:S(2)}) copy-start(f32[64,1024]{1,0:T(8,128)} %weight_ref.1) | copy-start | bytes 786436
  73.8 2.2 %copy-start = (f32[16,121,512]{2,1,0:T(8,128)S(1)}, f32[16,121,512]{2,1,0:T(8,128)}, u32[]{:S(2)}) copy-start(f32[16,121,512]{2,1,0:T(8,128)} %all-gather.5.cloned.1.call-done.cells_ref) | copy-start | bytes 11894788
Sparse Core Ops, SparseCore 0:
  10.1 62.1 all-gather.4

commit v2 on v1

--- a/solution.py
+++ b/solution.py
@@ -8,6 +8,7 @@
 ORDER = 10
 HALO = 16
 WIDE = 128
+PACK = 64
 F32 = jnp.float32
 BF16 = jnp.bfloat16
 NT = (((1,), (1,)), ((), ()))
@@ -94,7 +95,7 @@
 
 
 def far_kernel(top_ref, weight_ref, far_ref, shift_ref, place_ref, near_ref, out_ref):
-    top = jnp.concatenate([top_ref[0][:, None], top_ref[1][:, None]], axis=1)
+    top = jnp.concatenate([top_ref[:, 0][:, :, None], top_ref[:, 1][:, :, None]], axis=2)
     top = top.reshape(-1, WIDE)
     summed = dot_exact(weight_ref[...], top, NN)
     parent = dot_exact(summed, far_ref[...], NT)
@@ -109,38 +110,82 @@
         out_ref[at : at + slots, :] = near_ref[at : at + slots, :] + halves(picked)
 
 
-def pair_kernel(cells_ref, source_ref, target_ref, operator_ref, near_ref, out_ref, block, moved, total):
-    peer = pl.program_id(0)
+def positions(ids):
+    slots = ids.shape[1]
+    used = ids >= 0.0
+    row = lax.broadcasted_iota(jnp.int32, (slots, slots), 0)
+    lane = lax.broadcasted_iota(jnp.int32, (slots, slots), 1)
+    earlier = jnp.where(row < lane, 1.0, 0.0).astype(BF16)
+    place = dot(jnp.where(used, 1.0, 0.0).astype(BF16), earlier, NN)
+    return jnp.where(used, place, -1.0)
+
+
+def digits(ids):
+    value = ids + 1.0
+    high = jnp.floor(value * (1.0 / 32.0))
+    return high, value - 32.0 * high
+
+
+def translate_and_pack(cells_ref, by_offset_ref, ids, operator_ref, block, terms, signed, store):
+    coefs, cells = cells_ref.shape
+    offsets = operator_ref.shape[0]
+    peers = ids.shape[0]
+    sign = degree_signs(WIDE)
+    block[...] = jnp.zeros_like(block)
+    block[:coefs, :] = cells_ref[...]
+    held = both_terms(block[...], 0)
+    for o in range(offsets):
+        picked = halves(dot(source_indicator(by_offset_ref[o : o + 1, :], cells), held, NT))
+        if signed:
+            picked = picked * sign
+        moved = translate(picked, operator_ref[o])
+        if signed:
+            moved = moved * sign
+        terms[:, o] = moved.reshape(peers, -1, WIDE)
+    place = positions(ids)
+    high, low = digits(ids)
+    packed = []
+    for p in range(peers):
+        pick = target_indicator(place[p : p + 1, :], PACK)
+        store(p, halves(dot(pick, both_terms(terms[p].reshape(-1, WIDE), 1), NN)))
+        both = jnp.concatenate([high[p : p + 1], low[p : p + 1]], axis=0).astype(BF16)
+        both = dot(both, pick, NT)
+        packed.append(32.0 * both[:1] + both[1:] - 1.0)
+    return jnp.concatenate(packed, axis=0)
+
+
+def listed_kernel(cells_ref, by_offset_ref, ids_ref, operator_ref, out_ref, packed_ref, block, terms):
+    def store(p, value):
+        out_ref[p] = value
+
+    packed_ref[...] = translate_and_pack(
+        cells_ref, by_offset_ref, ids_ref[...], operator_ref, block, terms, False, store
+    )
+
+
+def answer_kernel(
+    cells_ref, by_offset_ref, ids_ref, operator_ref, listed_ref, listed_ids_ref, out_ref, packed_ref, block, terms
+):
+    def store(p, value):
+        out_ref[p, :PACK] = listed_ref[p]
+        out_ref[p, PACK:] = value
+
+    packed = translate_and_pack(
+        cells_ref, by_offset_ref, ids_ref[...], operator_ref, block, terms, True, store
+    )
+    packed_ref[...] = jnp.concatenate([packed, listed_ids_ref[...]], axis=1)
+
+
+def sum_kernel(terms_ref, target_ref, near_ref, out_ref, total):
     coefs, cells = out_ref.shape
-    offsets = operator_ref.shape[0]
-    sign = degree_signs(WIDE)
-
-    @pl.when(peer == 0)
-    def _():
-        block[...] = jnp.zeros_like(block)
-
-    block[:coefs, :] = cells_ref[0]
-    held = both_terms(block[...], 0)
-    for way in range(2):
-        picked = halves(dot(source_indicator(source_ref[0, way : way + 1, :], cells), held, NT))
-        if way == 1:
-            picked = picked * sign
-        moved[:, way, peer] = picked.reshape(offsets, -1, WIDE)
-
-    @pl.when(peer == pl.num_programs(0) - 1)
-    def _():
-        total[...] = jnp.zeros_like(total)
-        for o in range(offsets):
-            terms = translate(moved[o].reshape(-1, WIDE), operator_ref[o])
-            count = terms.shape[0] // 2
-            terms = jnp.concatenate([terms[:count], terms[count:] * sign], axis=0)
-            total[...] += dot(target_indicator(target_ref[o : o + 1, :], cells), both_terms(terms, 1), NN)
-        result = near_ref[...] + halves(total[...])
-        out_ref[...] = jnp.transpose(result)[:coefs, :]
-
-
-def whole(shape):
-    return pl.BlockSpec(shape, lambda *_: (0,) * len(shape))
+    peers = terms_ref.shape[0]
+    total[...] = jnp.zeros_like(total)
+    for p in range(0, peers, 2):
+        terms = jnp.concatenate([terms_ref[p], terms_ref[p + 1]], axis=0)
+        target = jnp.concatenate([target_ref[p : p + 1, :], target_ref[p + 1 : p + 2, :]], axis=1)
+        total[...] += dot(target_indicator(target, cells), both_terms(terms, 1), NN)
+    result = near_ref[...] + halves(total[...])
+    out_ref[...] = jnp.transpose(result)[:coefs, :]
 
 
 def body(
@@ -165,27 +210,33 @@
     segs = lax.axis_size("seg")
     params = pltpu.CompilerParams(vmem_limit_bytes=48 * 1024 * 1024)
 
-    group = lax.all_gather(multipoles, "sub", axis=0, tiled=False)
-
     used = lax.broadcasted_iota(jnp.int32, (peers, offsets, room), 2) < pair_counts[0][..., None]
-    own_source = jnp.where(used, pair_sources[0], -1).reshape(peers, slots).astype(F32)
     own_target = jnp.where(used, peer_target_cells[0], -1).reshape(peers, slots).astype(F32)
     top = jnp.broadcast_to(jnp.pad(top_multipoles[:, 0], (0, pad))[None], (peers, WIDE))
-    message = jnp.stack([own_source, own_target, top], axis=1)
+    message = jnp.stack([own_target, top], axis=1)
     arrived = lax.all_to_all(message, "sub", split_axis=0, concat_axis=0, tiled=True)
-    their_source, their_target, tops = arrived[:, 0], arrived[:, 1], arrived[:, 2]
-
+    their_target, tops = arrived[:, 0], arrived[:, 1]
+
+    ys = 1
+    while ys * ys < segs:
+        ys *= 2
+    xs = segs // ys
     core = lax.axis_index("sub") % 2
     half = peers // 2
     mine = lax.dynamic_slice_in_dim(tops, core * half, half, axis=0)
     spread = lax.all_to_all(
-        jnp.broadcast_to(mine[None], (segs, half, WIDE)), "seg", split_axis=0, concat_axis=0, tiled=True
-    )
-    every_top = lax.all_gather(
+        jnp.broadcast_to(mine[None], (ys, half, WIDE)),
+        "seg",
+        split_axis=0,
+        concat_axis=0,
+        tiled=True,
+        axis_index_groups=[[x * ys + y for y in range(ys)] for x in range(xs)],
+    )
+    shared = lax.all_gather(
         spread,
         "sub",
         axis=0,
-        tiled=False,
+        tiled=True,
         axis_index_groups=[[2 * i, 2 * i + 1] for i in range(half)],
     )
 
@@ -198,6 +249,49 @@
     window = jnp.pad(window, ((0, pad), (0, span - window.shape[1])))
 
     operators = jnp.pad(translators, ((0, 0), (0, pad), (0, pad)))
+
+    def by_offset(ids):
+        return ids.reshape(peers, offsets, room).transpose(1, 0, 2).reshape(offsets, -1)
+
+    own_source = jnp.where(used, pair_sources[0], -1).reshape(peers, slots).astype(F32)
+    scratch = [pltpu.VMEM((WIDE, cells), F32), pltpu.VMEM((peers, offsets, room, WIDE), F32)]
+    pair_cost = pl.CostEstimate(flops=4 * 10**9, bytes_accessed=3 * 10**6, transcendentals=0)
+    listed, listed_ids = pl.pallas_call(
+        listed_kernel,
+        out_shape=(
+            jax.ShapeDtypeStruct((peers, PACK, WIDE), F32),
+            jax.ShapeDtypeStruct((peers, PACK), F32),
+        ),
+        scratch_shapes=scratch,
+        compiler_params=params,
+        cost_estimate=pair_cost,
+        name="listed_terms",
+    )(multipoles, by_offset(own_source), own_source, operators)
+    packet, targets = pl.pallas_call(
+        answer_kernel,
+        out_shape=(
+            jax.ShapeDtypeStruct((peers, 2 * PACK, WIDE), F32),
+            jax.ShapeDtypeStruct((peers, 2 * PACK), F32),
+        ),
+        scratch_shapes=scratch,
+        compiler_params=params,
+        cost_estimate=pair_cost,
+        name="answers",
+    )(multipoles, by_offset(their_target), their_target, operators, listed, listed_ids)
+    packet, shared = lax.optimization_barrier((packet, shared))
+    received = lax.all_to_all(packet, "sub", split_axis=0, concat_axis=0, tiled=True)
+
+    every_top = shared.reshape(1, 2 * ys * half, WIDE)
+    if xs > 1:
+        every_top = lax.all_gather(
+            every_top,
+            "seg",
+            axis=0,
+            tiled=True,
+            axis_index_groups=[[x * ys + y for x in range(xs)] for y in range(ys)],
+        )
+    every_top = every_top.reshape(xs, 2, ys, half, WIDE)
+
     shifts = jnp.pad(child_shifts, ((0, 0), (0, pad), (0, pad)))
     far = jnp.pad(far_operator, ((0, pad), (0, pad)))
 
@@ -229,30 +323,14 @@
         name="far_field",
     )(every_top, far_weights, far, shifts, place, near)
 
-    sources = jnp.stack([their_source, own_target], axis=1)
-    targets = jnp.stack([their_target, own_source], axis=0)
-    targets = targets.reshape(2, peers, offsets, room).transpose(2, 0, 1, 3).reshape(offsets, -1)
     return pl.pallas_call(
-        pair_kernel,
-        grid=(peers,),
-        in_specs=[
-            pl.BlockSpec((1, coefs, cells), lambda p: (p, 0, 0)),
-            pl.BlockSpec((1, 2, slots), lambda p: (p, 0, 0)),
-            whole(targets.shape),
-            whole(operators.shape),
-            whole(near.shape),
-        ],
-        out_specs=whole((coefs, cells)),
+        sum_kernel,
         out_shape=jax.ShapeDtypeStruct((coefs, cells), F32),
-        scratch_shapes=[
-            pltpu.VMEM((WIDE, cells), F32),
-            pltpu.VMEM((offsets, 2, peers, room, WIDE), F32),
-            pltpu.VMEM((cells, 2 * WIDE), F32),
-        ],
-        compiler_params=params,
-        cost_estimate=pl.CostEstimate(flops=6 * 10**9, bytes_accessed=6 * 10**6, transcendentals=0),
-        name="pair_terms",
-    )(group, sources, targets, operators, near)
+        scratch_shapes=[pltpu.VMEM((cells, 2 * WIDE), F32)],
+        compiler_params=params,
+        cost_estimate=pl.CostEstimate(flops=2 * 10**9, bytes_accessed=3 * 10**6, transcendentals=0),
+        name="sum_terms",
+    )(received, targets, near)
 
 
 def solution(mesh):

time: 92.8 us -> 101 us (1.088)
  the two profiles are of different devices: /device:TPU:1 before, /device:TPU:118 now
where the time goes in v2:
time: 101 us; the launch traced here: 100 us
  starting transfers between devices  37.6 us (37%)
  blocking collectives  27.4 us (27%)
  Pallas kernels  19.5 us (19%)
  local copies, waits for them, and re-layouts  8.32 us (8%)
  waiting for transfers between devices  5.76 us (6%)
  other arithmetic  1.16 us (1%)
    all_gather x1, blocking collectives, body(): lax.all_gather(every_top, 'seg', axis=0, tiled=True, axis_index_groups=[[...  25.5 us
    all_to_all x1, starting transfers between devices, body(): lax.all_to_all(message, 'sub', split_axis=0, concat_axis=0, tiled=True)  16.8 us
    all_to_all x1, starting transfers between devices, body(): lax.all_to_all(packet, 'sub', split_axis=0, concat_axis=0, tiled=True)  7.34 us
    pallas_call x1, Pallas kernels, body(): pl.pallas_call(answer_kernel, out_shape=(jax.ShapeDtypeStruct((peers, 2 *...  6.92 us
    all_to_all x1, starting transfers between devices, body(): lax.all_to_all(jnp.broadcast_to(mine[None], (ys, half, WIDE)), 'seg', spl...  6.52 us
    pallas_call x1, Pallas kernels, body(): pl.pallas_call(listed_kernel, out_shape=(jax.ShapeDtypeStruct((peers, PAC...  5.89 us
    ppermute x1, waiting for transfers between devices, body(): after = lax.ppermute(multipoles[:, :HALO], 'seg', down)  5.74 us
    unnamed x23, local copies, waits for them, and re-layouts  5.39 us
  transfers between devices with their start and end apart: 5, of which 1 were waited for; matrix products, arithmetic and copies ran while one was open for 3% of the time, Pallas kernels for 18%

profile of v2, /device:TPU:118, one launch (start us, length us, event | category | flops | bytes accessed | tf_op | source)
XLA Modules:
  0.0 100.0 jit_solution(10989745246481542701)
XLA Ops:
  0.0 0.9 copy.79
  0.9 0.1 iota.23
  0.9 0.9 copy.65
  1.9 0.7 pad.20
  2.5 0.1 fusion.2
  2.6 0.1 stack_broadcast_in_dim.2
  2.7 0.7 copy.66
  3.4 16.8 %all-to-all-start = ((f32[16,2,128]{2,1,0:T(2,128)}), f32[16,2,128]{2,1,0:T(2,128)S(1)}, u32[]{:S(2)}, u32[]{:S(2)}) async-start(f32[16,2,128]{2,1,0:T(2,128)} %copy.66), calls=%async_computation | async-start | bytes 32768 | tf_op jit(solution)/shard_map/all_to_all | solution.py:217
  20.2 0.0 copy-start.5
  20.2 0.9 copy.73
  21.2 0.9 fusion.1
  22.0 0.1 copy.72
  22.1 0.1 copy.74
  22.2 0.3 copy.70
  22.5 0.0 copy-start
  22.5 0.1 pad.21.operator_ref
  22.6 0.1 copy.75.by_offset_ref
  22.7 0.8 copy-done
  23.5 5.9 %listed_terms.1 = (f32[16,64,128]{2,1,0:T(8,128)S(1)}, f32[16,64]{1,0:T(8,128)S(1)}) custom-call(f32[121,512]{1,0:T(8,128)S(1)} %copy-done, f32[16,128]{1,0:T(8,128)S(1)} %copy.75.by_offset_ref, f32[16,128]{1,0:T(8,128)S(1)} %select_convert_fusion.ids_ref, f32[16,128,128]{2,1,0:T(8,128)S(1)} %pad.21.operator_ref), custom_call_target="tpu_custom_call" | custom-call | flops 4000000000 | bytes 3000000 | tf_op jit(solution)/shard_map/listed_terms/pallas_call | solution.py:259
  29.4 0.0 all-to-all-done
  29.4 0.6 broadcast_in_dim.22
  30.0 6.5 %all-to-all-start.1 = ((f32[8,8,128]{2,1,0:T(8,128)}), f32[8,8,128]{2,1,0:T(8,128)S(1)}, u32[]{:S(2)}, u32[]{:S(2)}) async-start(f32[8,8,128]{2,1,0:T(8,128)} %broadcast_in_dim.22), calls=%async_computation.1 | async-start | bytes 65536 | tf_op jit(solution)/shard_map/all_to_all | solution.py:227
  36.6 0.1 copy.68
  36.7 0.1 copy.69
  36.8 0.1 copy.76.by_offset_ref
  36.8 6.9 %answers.1 = (f32[16,128,128]{2,1,0:T(8,128)}, f32[16,128]{1,0:T(8,128)S(1)}) custom-call(f32[121,512]{1,0:T(8,128)S(1)} %copy-done, f32[16,128]{1,0:T(8,128)S(1)} %copy.76.by_offset_ref, f32[16,128]{1,0:T(8,128)S(1)} %bitcast.35, f32[16,128,128]{2,1,0:T(8,128)S(1)} %pad.21.operator_ref, f32[16,64,128]{2,1,0:T(8,128)S(1)} %get-tuple-element.11.listed_ref, ...), custom_call_target="tpu_custom_call" | custom-call | flops 4000000000 | bytes 3000000 | tf_op jit(solution)/shard_map/answers/pallas_call | solution.py:270
  43.7 0.0 all-to-all-done.1
  43.7 1.8 %all_gather.6 = f32[16,8,128]{2,1,0:T(8,128)S(1)} all-gather(f32[8,8,128]{2,1,0:T(8,128)S(1)} %all-to-all-done.1), channel_id=1, replica_groups={{0,1},{2,3},{4,5},{6,7},{8,9},{10,11},{12,13},{14,15},{16,17},{18,19},{..., dimensions={0}, use_global_device_ids=true | all-gather | bytes 98304 | tf_op jit(solution)/shard_map/all_gather | solution.py:235
  45.6 7.3 %all-to-all-start.2 = ((f32[16,128,128]{2,1,0:T(8,128)}), f32[16,128,128]{2,1,0:T(8,128)S(1)}, u32[]{:S(2)}, u32[]{:S(2)}) async-start(f32[16,128,128]{2,1,0:T(8,128)} %get-tuple-element.14), calls=%async_computation.2 | async-start | bytes 2097152 | tf_op jit(solution)/shard_map/all_to_all | solution.py:282
  52.9 0.0 copy-start.6
  52.9 0.1 fusion.6
  53.0 5.0 %collective-permute-start = (f32[121,16]{1,0:T(8,128)S(1)}, f32[121,16]{1,0:T(8,128)S(1)}, u32[]{:S(2)}, u32[]{:S(2)}) collective-permute-start(f32[121,16]{1,0:T(8,128)S(1)} %get-tuple-element.17), channel_id=1, source_target_pairs={{0,16},{16,32},{32,48},{48,64},{64,80},{80,96},{96,112},{112,128},... | collective-permute-start | bytes 23240 | tf_op jit(solution)/shard_map/ppermute | solution.py:245
  58.1 1.9 %collective-permute-start.1 = (f32[121,16]{1,0:T(8,128)S(1)}, f32[121,16]{1,0:T(8,128)S(1)}, u32[]{:S(2)}, u32[]{:S(2)}) collective-permute-start(f32[121,16]{1,0:T(8,128)S(1)} %get-tuple-element.18), channel_id=1, source_target_pairs={{16,0},{32,16},{48,32},{64,48},{80,64},{96,80},{112,96},{128,112},... | collective-permute-start | bytes 23240 | tf_op jit(solution)/shard_map/ppermute | solution.py:246
  60.1 0.0 copy-start.7
  60.1 0.1 convert_element_type.43.source_ref
  60.1 0.6 copy-done.7
  60.8 0.1 convert_element_type.45.target_ref
  60.8 0.1 copy.77
  60.9 0.0 copy-start.4
  61.0 0.8 copy-done.4
  61.8 5.7 %collective-permute-done.1 = f32[121,16]{1,0:T(8,128)S(1)} collective-permute-done((f32[121,16]{1,0:T(8,128)S(1)}, f32[121,16]{1,0:T(8,128)S(1)}, u32[]{:S(2)}, u32[]{:S(2)}) %collective-permute-start.1) | collective-permute-done | bytes 7776 | tf_op jit(solution)/shard_map/ppermute | solution.py:246
  67.6 0.2 select_maximum_fusion.window_ref
  67.7 3.2 %inner_pairs.1.near_ref = f32[512,128]{1,0:T(8,128)S(1)} custom-call(f32[128,640]{1,0:T(8,128)S(1)} %select_maximum_fusion.window_ref, f32[8,128]{1,0:T(8,128)S(1)} %convert_element_type.43.source_ref, f32[8,128]{1,0:T(8,128)S(1)} %convert_element_type.45.target_ref, f32[16,128,128]{2,1,0:T(8,128)S(1)} %pad.21.operator_ref), custom_call_target="tpu_custom_call" | custom-call | flops 2000000000 | bytes 3000000 | tf_op jit(solution)/shard_map/inner_pairs/pallas_call | solution.py:299
  70.9 0.0 copy-start.1
  70.9 25.5 %all_gather.7 = f32[8,128,128]{2,1,0:T(8,128)S(1)} all-gather(f32[1,128,128]{2,1,0:T(8,128)S(1)} %bitcast.36), channel_id=1, replica_groups={{0,128,256,384,512,640,768,896},{16,144,272,400,528,656,784,912},{32,16..., dimensions={0}, use_global_device_ids=true | all-gather | bytes 589824 | tf_op jit(solution)/shard_map/all_gather | solution.py:286
  96.5 2.1 %far_field.1.near_ref = f32[512,128]{1,0:T(8,128)S(1)} custom-call(f32[8,2,8,8,128]{4,3,2,1,0:T(8,128)S(1)} %bitcast.33, f32[64,1024]{1,0:T(8,128)S(1)} %copy-done.1, f32[128,128]{1,0:T(8,128)S(1)} %pad.22.far_ref, f32[8,128,128]{2,1,0:T(8,128)S(1)} %pad.23.shift_ref, f32[1,512]{1,0:T(1,128)S(1)} %fusion.5.place_ref, f32[512,128]{1,0:T(8,128)S(1)} %inner_pairs.1.near_ref), custom_call_target="tpu_custom_call" | custom-call | flops 1000000000 | bytes 2000000 | tf_op jit(solution)/shard_map/far_field/pallas_call | solution.py:318
  98.5 0.0 all-to-all-done.2.terms_ref
  98.5 1.5 %sum_terms.1 = f32[121,512]{1,0:T(8,128)} custom-call(f32[16,128,128]{2,1,0:T(8,128)S(1)} %all-to-all-done.2.terms_ref, f32[16,128]{1,0:T(8,128)S(1)} %get-tuple-element.15.target_ref, f32[512,128]{1,0:T(8,128)S(1)} %far_field.1.near_ref), custom_call_target="tpu_custom_call" | custom-call | flops 2000000000 | bytes 3000000 | tf_op jit(solution)/shard_map/sum_terms/pallas_call | solution.py:326
  (21 shorter events, 0.2 us)
Async XLA Ops:
  0.0 22.2 %copy-start.2 = (f32[16,121,121]{2,0,1:T(8,128)S(1)}, f32[16,121,121]{2,0,1:T(8,128)}, u32[]{:S(2)}) copy-start(f32[16,121,121]{2,0,1:T(8,128)} %param.14) | copy-start | bytes 2811076
  3.4 26.0 %all-to-all-start = ((f32[16,2,128]{2,1,0:T(2,128)}), f32[16,2,128]{2,1,0:T(2,128)S(1)}, u32[]{:S(2)}, u32[]{:S(2)}) async-start(f32[16,2,128]{2,1,0:T(2,128)} %copy.66), calls=%async_computation | async-start | bytes 32768 | tf_op jit(solution)/shard_map/all_to_all | solution.py:217
  20.2 1.0 copy-start.5
  22.5 1.0 copy-start
  30.0 13.7 %all-to-all-start.1 = ((f32[8,8,128]{2,1,0:T(8,128)}), f32[8,8,128]{2,1,0:T(8,128)S(1)}, u32[]{:S(2)}, u32[]{:S(2)}) async-start(f32[8,8,128]{2,1,0:T(8,128)} %broadcast_in_dim.22), calls=%async_computation.1 | async-start | bytes 65536 | tf_op jit(solution)/shard_map/all_to_all | solution.py:227
  45.6 15.3 %copy-start.3 = (f32[8,121,121]{2,0,1:T(8,128)S(1)}, f32[8,121,121]{2,0,1:T(8,128)}, u32[]{:S(2)}) copy-start(f32[8,121,121]{2,0,1:T(8,128)} %param.15) | copy-start | bytes 1405540
  45.6 52.9 %all-to-all-start.2 = ((f32[16,128,128]{2,1,0:T(8,128)}), f32[16,128,128]{2,1,0:T(8,128)S(1)}, u32[]{:S(2)}, u32[]{:S(2)}) async-start(f32[16,128,128]{2,1,0:T(8,128)} %get-tuple-element.14), calls=%async_computation.2 | async-start | bytes 2097152 | tf_op jit(solution)/shard_map/all_to_all | solution.py:282
  52.9 7.1 %copy-start.6 = (s32[1,16,64]{2,1,0:T(8,128)S(1)}, s32[1,16,64]{2,1,0:T(8,128)}, u32[]{:S(2)}) copy-start(s32[1,16,64]{2,1,0:T(8,128)} %param.19) | copy-start | bytes 12292
  53.0 7.0 %copy-start.8 = (s32[1,512]{1,0:T(1,128)S(1)}, s32[1,512]{1,0:T(1,128)}, u32[]{:S(2)}) copy-start(s32[1,512]{1,0:T(1,128)} %param.18) | copy-start | bytes 6148
  53.0 8.8 %collective-permute-start = (f32[121,16]{1,0:T(8,128)S(1)}, f32[121,16]{1,0:T(8,128)S(1)}, u32[]{:S(2)}, u32[]{:S(2)}) collective-permute-start(f32[121,16]{1,0:T(8,128)S(1)} %get-tuple-element.17), channel_id=1, source_target_pairs={{0,16},{16,32},{32,48},{48,64},{64,80},{80,96},{96,112},{112,128},... | collective-permute-start | bytes 23240 | tf_op jit(solution)/shard_map/ppermute | solution.py:245
  58.1 9.5 %collective-permute-start.1 = (f32[121,16]{1,0:T(8,128)S(1)}, f32[121,16]{1,0:T(8,128)S(1)}, u32[]{:S(2)}, u32[]{:S(2)}) collective-permute-start(f32[121,16]{1,0:T(8,128)S(1)} %get-tuple-element.18), channel_id=1, source_target_pairs={{16,0},{32,16},{48,32},{64,48},{80,64},{96,80},{112,96},{128,112},... | collective-permute-start | bytes 23240 | tf_op jit(solution)/shard_map/ppermute | solution.py:246
  60.1 0.7 copy-start.7
  60.9 0.8 copy-start.4
  70.9 25.5 %copy-start.1 = (f32[64,1024]{1,0:T(8,128)S(1)}, f32[64,1024]{1,0:T(8,128)}, u32[]{:S(2)}) copy-start(f32[64,1024]{1,0:T(8,128)} %weight_ref.1) | copy-start | bytes 786436

commit v3 on v2

--- a/solution.py
+++ b/solution.py
@@ -67,10 +67,18 @@
 
 def translate(columns, operator):
     high, low = two_terms(columns)
-    op_high, op_low = two_terms(operator)
-    return (
-        dot(high, op_high, NT) + dot(low, op_high, NT) + dot(high, op_low, NT)
-    )
+    return dot(jnp.concatenate([high, low, high], axis=1), operator, NN)
+
+
+def three_terms(operators):
+    pad = WIDE - operators.shape[1]
+    turned = jnp.pad(jnp.swapaxes(operators, 1, 2), ((0, 0), (0, pad), (0, pad)))
+    high = lax.reduce_precision(turned, 8, 7)
+    return jnp.concatenate([high, high, turned - high], axis=1).astype(BF16)
+
+
+def turned_terms(block):
+    return both_terms(jnp.transpose(block), 1)
 
 
 def inner_kernel(window_ref, source_ref, target_ref, operator_ref, out_ref, moved, total):
@@ -80,9 +88,9 @@
     slots = source_ref.shape[1]
     rows = source_ref.shape[0]
     each = rows * slots // offsets
-    window = both_terms(window_ref[...], 0)
+    window = turned_terms(window_ref[...])
     for r in range(rows):
-        picked = dot(source_indicator(source_ref[r : r + 1, :], span), window, NT)
+        picked = dot(source_indicator(source_ref[r : r + 1, :], span), window, NN)
         moved[r * slots : (r + 1) * slots, :] = halves(picked)
     total[...] = jnp.zeros_like(total)
     for r in range(rows):
@@ -95,7 +103,7 @@
 
 
 def far_kernel(top_ref, weight_ref, far_ref, shift_ref, place_ref, near_ref, out_ref):
-    top = jnp.concatenate([top_ref[:, 0][:, :, None], top_ref[:, 1][:, :, None]], axis=2)
+    top = jnp.concatenate([top_ref[0][:, None], top_ref[1][:, None]], axis=1)
     top = top.reshape(-1, WIDE)
     summed = dot_exact(weight_ref[...], top, NN)
     parent = dot_exact(summed, far_ref[...], NT)
@@ -120,60 +128,98 @@
     return jnp.where(used, place, -1.0)
 
 
-def digits(ids):
-    value = ids + 1.0
-    high = jnp.floor(value * (1.0 / 32.0))
-    return high, value - 32.0 * high
-
-
-def translate_and_pack(cells_ref, by_offset_ref, ids, operator_ref, block, terms, signed, store):
+def translate_and_pack(cells_ref, by_offset_ref, ids_ref, operator_ref, block, picked, terms, signed, store):
     coefs, cells = cells_ref.shape
-    offsets = operator_ref.shape[0]
-    peers = ids.shape[0]
+    offsets, slots = by_offset_ref.shape
+    peers = ids_ref.shape[0]
     sign = degree_signs(WIDE)
-    block[...] = jnp.zeros_like(block)
+    block[coefs // 8 * 8 :, :] = jnp.zeros((WIDE - coefs // 8 * 8, cells), F32)
     block[:coefs, :] = cells_ref[...]
-    held = both_terms(block[...], 0)
+    held = turned_terms(block[...])
+    for o in range(0, offsets, 2):
+        chosen = jnp.concatenate(
+            [source_indicator(by_offset_ref[i : i + 1, :], cells) for i in (o, o + 1)], axis=0
+        )
+        columns = halves(dot(chosen, held, NN))
+        picked[o * slots : (o + 2) * slots, :] = columns * sign if signed else columns
     for o in range(offsets):
-        picked = halves(dot(source_indicator(by_offset_ref[o : o + 1, :], cells), held, NT))
-        if signed:
-            picked = picked * sign
-        moved = translate(picked, operator_ref[o])
-        if signed:
-            moved = moved * sign
-        terms[:, o] = moved.reshape(peers, -1, WIDE)
-    place = positions(ids)
-    high, low = digits(ids)
-    packed = []
+        moved = translate(picked[o * slots : (o + 1) * slots, :], operator_ref[o])
+        terms[:, o] = (moved * sign if signed else moved).reshape(peers, -1, WIDE)
+    place = positions(ids_ref[...])
     for p in range(peers):
         pick = target_indicator(place[p : p + 1, :], PACK)
         store(p, halves(dot(pick, both_terms(terms[p].reshape(-1, WIDE), 1), NN)))
+
+
+def listed_kernel(cells_ref, by_offset_ref, ids_ref, operator_ref, out_ref, block, picked, terms):
+    def store(p, value):
+        out_ref[p] = value
+
+    translate_and_pack(
+        cells_ref, by_offset_ref, ids_ref, operator_ref, block, picked, terms, False, store
+    )
+
+
+def answer_kernel(
+    cells_ref, by_offset_ref, ids_ref, operator_ref, listed_ref, out_ref, block, picked, terms
+):
+    def store(p, value):
+        out_ref[p, :PACK] = listed_ref[p]
+        out_ref[p, PACK:] = value
+
+    translate_and_pack(
+        cells_ref, by_offset_ref, ids_ref, operator_ref, block, picked, terms, True, store
+    )
+
+
+def pack_ids(ids):
+    place = positions(ids)
+    value = ids + 1.0
+    high = jnp.floor(value * (1.0 / 32.0))
+    low = value - 32.0 * high
+    packed = []
+    for p in range(ids.shape[0]):
+        pick = target_indicator(place[p : p + 1, :], PACK)
         both = jnp.concatenate([high[p : p + 1], low[p : p + 1]], axis=0).astype(BF16)
         both = dot(both, pick, NT)
         packed.append(32.0 * both[:1] + both[1:] - 1.0)
     return jnp.concatenate(packed, axis=0)
 
 
-def listed_kernel(cells_ref, by_offset_ref, ids_ref, operator_ref, out_ref, packed_ref, block, terms):
-    def store(p, value):
-        out_ref[p] = value
-
-    packed_ref[...] = translate_and_pack(
-        cells_ref, by_offset_ref, ids_ref[...], operator_ref, block, terms, False, store
-    )
-
-
-def answer_kernel(
-    cells_ref, by_offset_ref, ids_ref, operator_ref, listed_ref, listed_ids_ref, out_ref, packed_ref, block, terms
-):
-    def store(p, value):
-        out_ref[p, :PACK] = listed_ref[p]
-        out_ref[p, PACK:] = value
-
-    packed = translate_and_pack(
-        cells_ref, by_offset_ref, ids_ref[...], operator_ref, block, terms, True, store
-    )
-    packed_ref[...] = jnp.concatenate([packed, listed_ids_ref[...]], axis=1)
+def target_kernel(their_ref, own_ref, out_ref):
+    out_ref[...] = jnp.concatenate([pack_ids(their_ref[...]), pack_ids(own_ref[...])], axis=1)
+
+
+def spread_ids(ids, counts):
+    peers, offsets, room = ids.shape
+    slots = offsets * room
+    value = ids.reshape(peers * offsets, room).astype(F32)
+    high = jnp.floor(value * (1.0 / 32.0))
+    both = jnp.concatenate([high, value - 32.0 * high], axis=0).astype(BF16)
+    row = lax.broadcasted_iota(jnp.int32, (room, slots), 0)
+    lane = lax.broadcasted_iota(jnp.int32, (room, slots), 1)
+    wide = dot(both, jnp.where(lane % room == row, 1.0, 0.0).astype(BF16), NN)
+    wide = 32.0 * wide[: peers * offsets] + wide[peers * offsets :]
+    wide = wide.reshape(peers, offsets, slots)
+    row = lax.broadcasted_iota(jnp.int32, wide.shape, 1)
+    lane = lax.broadcasted_iota(jnp.int32, wide.shape, 2)
+    flat = jnp.sum(jnp.where(lane // room == row, wide, 0.0), axis=1)
+    row = lax.broadcasted_iota(jnp.int32, (offsets, slots), 0)
+    lane = lax.broadcasted_iota(jnp.int32, (offsets, slots), 1)
+    count = dot(counts.astype(F32).astype(BF16), jnp.where(lane // room == row, 1.0, 0.0).astype(BF16), NN)
+    slot = lax.broadcasted_iota(jnp.int32, flat.shape, 1) % room
+    return jnp.where(slot.astype(F32) < count, flat, -1.0)
+
+
+def message_kernel(source_ref, target_ref, count_ref, top_ref, out_ref, own_source_ref):
+    peers = target_ref.shape[0]
+    counts = count_ref[...]
+    coefs = top_ref.shape[1]
+    own_source_ref[...] = spread_ids(source_ref[...], counts)
+    own_target = spread_ids(target_ref[...], counts)
+    out_ref[:, 1, :coefs] = jnp.broadcast_to(top_ref[...], (peers, coefs))
+    out_ref[:, 1, coefs:] = jnp.zeros((peers, WIDE - coefs), F32)
+    out_ref[:, 0, :] = own_target
 
 
 def sum_kernel(terms_ref, target_ref, near_ref, out_ref, total):
@@ -210,34 +256,23 @@
     segs = lax.axis_size("seg")
     params = pltpu.CompilerParams(vmem_limit_bytes=48 * 1024 * 1024)
 
-    used = lax.broadcasted_iota(jnp.int32, (peers, offsets, room), 2) < pair_counts[0][..., None]
-    own_target = jnp.where(used, peer_target_cells[0], -1).reshape(peers, slots).astype(F32)
-    top = jnp.broadcast_to(jnp.pad(top_multipoles[:, 0], (0, pad))[None], (peers, WIDE))
-    message = jnp.stack([own_target, top], axis=1)
+    message, own_source = pl.pallas_call(
+        message_kernel,
+        out_shape=(
+            jax.ShapeDtypeStruct((peers, 2, WIDE), F32),
+            jax.ShapeDtypeStruct((peers, slots), F32),
+        ),
+        compiler_params=params,
+        name="message",
+    )(pair_sources[0], peer_target_cells[0], pair_counts[0], top_multipoles.reshape(1, coefs))
     arrived = lax.all_to_all(message, "sub", split_axis=0, concat_axis=0, tiled=True)
     their_target, tops = arrived[:, 0], arrived[:, 1]
 
-    ys = 1
-    while ys * ys < segs:
-        ys *= 2
-    xs = segs // ys
     core = lax.axis_index("sub") % 2
     half = peers // 2
     mine = lax.dynamic_slice_in_dim(tops, core * half, half, axis=0)
     spread = lax.all_to_all(
-        jnp.broadcast_to(mine[None], (ys, half, WIDE)),
-        "seg",
-        split_axis=0,
-        concat_axis=0,
-        tiled=True,
-        axis_index_groups=[[x * ys + y for y in range(ys)] for x in range(xs)],
-    )
-    shared = lax.all_gather(
-        spread,
-        "sub",
-        axis=0,
-        tiled=True,
-        axis_index_groups=[[2 * i, 2 * i + 1] for i in range(half)],
+        jnp.broadcast_to(mine[None], (segs, half, WIDE)), "seg", split_axis=0, concat_axis=0, tiled=True
     )
 
     up = [(i, i + 1) for i in range(segs - 1)]
@@ -248,49 +283,48 @@
     span = cells + WIDE
     window = jnp.pad(window, ((0, pad), (0, span - window.shape[1])))
 
-    operators = jnp.pad(translators, ((0, 0), (0, pad), (0, pad)))
+    operators = three_terms(translators)
 
     def by_offset(ids):
         return ids.reshape(peers, offsets, room).transpose(1, 0, 2).reshape(offsets, -1)
 
-    own_source = jnp.where(used, pair_sources[0], -1).reshape(peers, slots).astype(F32)
-    scratch = [pltpu.VMEM((WIDE, cells), F32), pltpu.VMEM((peers, offsets, room, WIDE), F32)]
-    pair_cost = pl.CostEstimate(flops=4 * 10**9, bytes_accessed=3 * 10**6, transcendentals=0)
-    listed, listed_ids = pl.pallas_call(
+    scratch = [
+        pltpu.VMEM((WIDE, cells), F32),
+        pltpu.VMEM((offsets * peers * room, WIDE), F32),
+        pltpu.VMEM((peers, offsets, room, WIDE), F32),
+    ]
+    pair_cost = pl.CostEstimate(flops=2 * 10**9, bytes_accessed=3 * 10**6, transcendentals=0)
+    listed = pl.pallas_call(
         listed_kernel,
-        out_shape=(
-            jax.ShapeDtypeStruct((peers, PACK, WIDE), F32),
-            jax.ShapeDtypeStruct((peers, PACK), F32),
-        ),
+        out_shape=jax.ShapeDtypeStruct((peers, PACK, WIDE), F32),
         scratch_shapes=scratch,
         compiler_params=params,
         cost_estimate=pair_cost,
         name="listed_terms",
     )(multipoles, by_offset(own_source), own_source, operators)
-    packet, targets = pl.pallas_call(
+    packet = pl.pallas_call(
         answer_kernel,
-        out_shape=(
-            jax.ShapeDtypeStruct((peers, 2 * PACK, WIDE), F32),
-            jax.ShapeDtypeStruct((peers, 2 * PACK), F32),
-        ),
+        out_shape=jax.ShapeDtypeStruct((peers, 2 * PACK, WIDE), F32),
         scratch_shapes=scratch,
         compiler_params=params,
         cost_estimate=pair_cost,
         name="answers",
-    )(multipoles, by_offset(their_target), their_target, operators, listed, listed_ids)
-    packet, shared = lax.optimization_barrier((packet, shared))
+    )(multipoles, by_offset(their_target), their_target, operators, listed)
+    packet, spread = lax.optimization_barrier((packet, spread))
     received = lax.all_to_all(packet, "sub", split_axis=0, concat_axis=0, tiled=True)
-
-    every_top = shared.reshape(1, 2 * ys * half, WIDE)
-    if xs > 1:
-        every_top = lax.all_gather(
-            every_top,
-            "seg",
-            axis=0,
-            tiled=True,
-            axis_index_groups=[[x * ys + y for x in range(xs)] for y in range(ys)],
-        )
-    every_top = every_top.reshape(xs, 2, ys, half, WIDE)
+    every_top = lax.all_gather(
+        spread,
+        "sub",
+        axis=0,
+        tiled=False,
+        axis_index_groups=[[2 * i, 2 * i + 1] for i in range(half)],
+    )
+    targets = pl.pallas_call(
+        target_kernel,
+        out_shape=jax.ShapeDtypeStruct((peers, 2 * PACK), F32),
+        compiler_params=params,
+        name="packed_targets",
+    )(their_target, own_source)
 
     shifts = jnp.pad(child_shifts, ((0, 0), (0, pad), (0, pad)))
     far = jnp.pad(far_operator, ((0, pad), (0, pad)))

time: 101 us -> 93.9 us (0.930)
  the two profiles are of different devices: /device:TPU:118 before, /device:TPU:1 now
where the time goes in v3:
time: 93.9 us; the launch traced here: 93.3 us
  starting transfers between devices  42.2 us (45%)
  waiting for transfers between devices  26.5 us (28%)
  Pallas kernels  11.8 us (13%)
  local copies, waits for them, and re-layouts  7.79 us (8%)
  blocking collectives  3.28 us (3%)
  other arithmetic  1.53 us (2%)
    all_to_all x1, starting transfers between devices, body(): lax.all_to_all(message, 'sub', split_axis=0, concat_axis=0, tiled=True)  18.2 us
    all_to_all x1, starting transfers between devices, body(): lax.all_to_all(jnp.broadcast_to(mine[None], (segs, half, WIDE)), 'seg', s...  13.3 us
    all_to_all x1, waiting for transfers between devices, body(): lax.all_to_all(packet, 'sub', split_axis=0, concat_axis=0, tiled=True)  9.4 us
    all_to_all x1, waiting for transfers between devices, body(): lax.all_to_all(jnp.broadcast_to(mine[None], (segs, half, WIDE)), 'seg', s...  8.24 us
    all_to_all x1, starting transfers between devices, body(): lax.all_to_all(packet, 'sub', split_axis=0, concat_axis=0, tiled=True)  6.34 us
    unnamed x26, local copies, waits for them, and re-layouts  5.65 us
    all_to_all x1, waiting for transfers between devices, body(): lax.all_to_all(message, 'sub', split_axis=0, concat_axis=0, tiled=True)  5.26 us
    ppermute x1, waiting for transfers between devices, body(): after = lax.ppermute(multipoles[:, :HALO], 'seg', down)  3.61 us
  transfers between devices with their start and end apart: 5, of which 4 were waited for; matrix products, arithmetic and copies ran while one was open for 5% of the time, Pallas kernels for 10%

profile of v3, /device:TPU:1, one launch (start us, length us, event | category | flops | bytes accessed | tf_op | source)
XLA Modules:
  0.0 93.3 jit_solution(5266932643376983957)
XLA Ops:
  0.0 0.9 copy.31
  0.9 0.9 copy.32
  1.9 0.0 copy-start.1
  1.9 0.7 copy-done.1
  2.6 0.7 copy-done.2
  3.2 0.9 message.1
  4.1 18.2 %all-to-all-start = ((f32[16,2,128]{2,1,0:T(2,128)}), f32[16,2,128]{2,1,0:T(2,128)S(1)}, u32[]{:S(2)}, u32[]{:S(2)}) async-start(f32[16,2,128]{2,1,0:T(2,128)} %get-tuple-element.9), calls=%async_computation | async-start | bytes 32768 | tf_op jit(solution)/shard_map/all_to_all | solution.py:268
  22.3 1.6 %copy.36 = f32[16,121,121]{1,2,0:T(8,128)S(1)} copy(f32[16,121,121]{2,0,1:T(8,128)} %param.14) | data formatting | bytes 1874048 | tf_op args[2]
  23.9 0.2 reduce-precision_convert_fusion
  24.1 0.1 copy.37
  24.2 0.1 copy.38
  24.3 0.1 copy.39.by_offset_ref
  24.4 5.3 %all-to-all-done = f32[16,2,128]{2,1,0:T(2,128)S(1)} async-done(((f32[16,2,128]{2,1,0:T(2,128)}), f32[16,2,128]{2,1,0:T(2,128)S(1)}, u32[]{:S(2)}, u32[]{:S(2)}) %all-to-all-start) | async-done | bytes 16416 | tf_op jit(solution)/shard_map/all_to_all | solution.py:268
  29.7 0.7 broadcast_in_dim.9
  30.4 13.3 %all-to-all-start.1 = ((f32[64,8,128]{2,1,0:T(8,128)}), f32[64,8,128]{2,1,0:T(8,128)S(1)}, u32[]{:S(2)}, u32[]{:S(2)}) async-start(f32[64,8,128]{2,1,0:T(8,128)} %broadcast_in_dim.9), calls=%async_computation.1 | async-start | bytes 524288 | tf_op jit(solution)/shard_map/all_to_all | solution.py:274
  43.7 0.3 pad_maximum_fusion.operator_ref
  44.0 0.0 copy-done
  44.0 1.6 %listed_terms.1.listed_ref = f32[16,64,128]{2,1,0:T(8,128)S(1)} custom-call(f32[121,512]{1,0:T(8,128)S(1)} %copy-done, f32[16,128]{1,0:T(8,128)S(1)} %copy.39.by_offset_ref, f32[16,128]{1,0:T(8,128)S(1)} %get-tuple-element.10.ids_ref.own_ref, bf16[16,384,128]{2,1,0:T(8,128)(2,1)S(1)} %pad_maximum_fusion.operator_ref), custom_call_target="tpu_custom_call" | custom-call | flops 2000000000 | bytes 3000000 | tf_op jit(solution)/shard_map/listed_terms/pallas_call | solution.py:297
  45.6 0.1 copy.34
  45.7 0.1 copy.35
  45.8 0.1 copy.40.by_offset_ref
  45.9 2.6 %answers.1 = f32[16,128,128]{2,1,0:T(8,128)} custom-call(f32[121,512]{1,0:T(8,128)S(1)} %copy-done, f32[16,128]{1,0:T(8,128)S(1)} %copy.40.by_offset_ref, f32[16,128]{1,0:T(8,128)S(1)} %bitcast.22, bf16[16,384,128]{2,1,0:T(8,128)(2,1)S(1)} %pad_maximum_fusion.operator_ref, f32[16,64,128]{2,1,0:T(8,128)S(1)} %listed_terms.1.listed_ref), custom_call_target="tpu_custom_call" | custom-call | flops 2000000000 | bytes 3000000 | tf_op jit(solution)/shard_map/answers/pallas_call | solution.py:305
  48.5 8.2 %all-to-all-done.1 = f32[64,8,128]{2,1,0:T(8,128)S(1)} async-done(((f32[64,8,128]{2,1,0:T(8,128)}), f32[64,8,128]{2,1,0:T(8,128)S(1)}, u32[]{:S(2)}, u32[]{:S(2)}) %all-to-all-start.1) | async-done | bytes 262176 | tf_op jit(solution)/shard_map/all_to_all | solution.py:274
  56.8 0.7 copy-done.4
  57.5 6.3 %all-to-all-start.2 = ((f32[16,128,128]{2,1,0:T(8,128)}), f32[16,128,128]{2,1,0:T(8,128)S(1)}, u32[]{:S(2)}, u32[]{:S(2)}) async-start(f32[16,128,128]{2,1,0:T(8,128)} %answers.1), calls=%async_computation.2 | async-start | bytes 2097152 | tf_op jit(solution)/shard_map/all_to_all | solution.py:314
  63.8 0.7 fusion.4
  64.5 3.0 %collective-permute-start = (f32[121,16]{1,0:T(8,128)}, f32[121,16]{1,0:T(8,128)}, u32[]{:S(2)}, u32[]{:S(2)}) collective-permute-start(f32[121,16]{1,0:T(8,128)} %get-tuple-element.15), channel_id=1, source_target_pairs={{0,16},{16,32},{32,48},{48,64},{64,80},{80,96},{96,112},{112,128},... | collective-permute-start | bytes 23240 | tf_op jit(solution)/shard_map/ppermute | solution.py:280
  67.5 1.3 %collective-permute-start.1 = (f32[121,16]{1,0:T(8,128)S(1)}, f32[121,16]{1,0:T(8,128)}, u32[]{:S(2)}, u32[]{:S(2)}) collective-permute-start(f32[121,16]{1,0:T(8,128)S(1)} %get-tuple-element.16), channel_id=1, source_target_pairs={{16,0},{32,16},{48,32},{64,48},{80,64},{96,80},{112,96},{128,112},... | collective-permute-start | bytes 23240 | tf_op jit(solution)/shard_map/ppermute | solution.py:281
  68.8 0.0 copy-done.10
  68.9 0.0 copy-done.8
  68.9 0.1 convert_element_type.24.source_ref
  68.9 0.0 copy-done.9
  69.0 0.1 convert_element_type.26.target_ref
  69.0 0.0 copy-done.6
  69.0 0.1 copy.41
  69.2 0.0 copy-done.7
  69.2 0.0 collective-permute-done
  69.2 3.6 %collective-permute-done.1 = f32[121,16]{1,0:T(8,128)} collective-permute-done((f32[121,16]{1,0:T(8,128)S(1)}, f32[121,16]{1,0:T(8,128)}, u32[]{:S(2)}, u32[]{:S(2)}) %collective-permute-start.1) | collective-permute-done | bytes 7776 | tf_op jit(solution)/shard_map/ppermute | solution.py:281
  72.8 1.0 %select_maximum_fusion.window_ref = f32[128,640]{1,0:T(8,128)S(1)} fusion(f32[121,16]{1,0:T(8,128)} %collective-permute-done.1, f32[121,512]{1,0:T(8,128)S(1)} %copy-done, f32[121,16]{1,0:T(8,128)} %collective-permute-done), kind=kLoop, calls=%fused_computation.4 | loop fusion | flops 901120 | bytes 590976 | tf_op jit(solution)/shard_map/concatenate | solution.py:282
  73.9 0.0 copy-start.5
  73.9 0.0 copy-start.3
  73.9 2.4 %inner_pairs.1.near_ref = f32[512,128]{1,0:T(8,128)S(1)} custom-call(f32[128,640]{1,0:T(8,128)S(1)} %select_maximum_fusion.window_ref, f32[8,128]{1,0:T(8,128)S(1)} %convert_element_type.24.source_ref, f32[8,128]{1,0:T(8,128)S(1)} %convert_element_type.26.target_ref, bf16[16,384,128]{2,1,0:T(8,128)(2,1)S(1)} %pad_maximum_fusion.operator_ref), custom_call_target="tpu_custom_call" | custom-call | flops 2000000000 | bytes 3000000 | tf_op jit(solution)/shard_map/inner_pairs/pallas_call | solution.py:333
  76.3 0.7 packed_targets.1.target_ref
  77.0 0.0 copy-done.5
  77.0 3.3 %all-gather = f32[128,8,128]{2,1,0:T(8,128)S(1)} all-gather(f32[64,8,128]{2,1,0:T(8,128)S(1)} %copy-done.5), channel_id=2, replica_groups={{0,1},{2,3},{4,5},{6,7},{8,9},{10,11},{12,13},{14,15},{16,17},{18,19},{..., dimensions={0}, use_global_device_ids=true | all-gather | bytes 786432 | tf_op jit(solution)/shard_map/all_gather | solution.py:315
  80.3 2.0 %far_field.1.near_ref = f32[512,128]{1,0:T(8,128)S(1)} custom-call(f32[2,64,8,128]{3,2,1,0:T(8,128)S(1)} %bitcast.18, f32[64,1024]{1,0:T(8,128)S(1)} %copy-done.3, f32[128,128]{1,0:T(8,128)S(1)} %pad.17.far_ref, f32[8,128,128]{2,1,0:T(8,128)S(1)} %pad.18.shift_ref, f32[1,512]{1,0:T(1,128)S(1)} %fusion.3.place_ref, f32[512,128]{1,0:T(8,128)S(1)} %inner_pairs.1.near_ref), custom_call_target="tpu_custom_call" | custom-call | flops 1000000000 | bytes 2000000 | tf_op jit(solution)/shard_map/far_field/pallas_call | solution.py:352
  82.4 9.4 %all-to-all-done.2.terms_ref = f32[16,128,128]{2,1,0:T(8,128)S(1)} async-done(((f32[16,128,128]{2,1,0:T(8,128)}), f32[16,128,128]{2,1,0:T(8,128)S(1)}, u32[]{:S(2)}, u32[]{:S(2)}) %all-to-all-start.2) | async-done | bytes 1048608 | tf_op jit(solution)/shard_map/all_to_all | solution.py:314
  91.8 1.5 %sum_terms.1 = f32[121,512]{1,0:T(8,128)} custom-call(f32[16,128,128]{2,1,0:T(8,128)S(1)} %all-to-all-done.2.terms_ref, f32[16,128]{1,0:T(8,128)S(1)} %packed_targets.1.target_ref, f32[512,128]{1,0:T(8,128)S(1)} %far_field.1.near_ref), custom_call_target="tpu_custom_call" | custom-call | flops 2000000000 | bytes 3000000 | tf_op jit(solution)/shard_map/sum_terms/pallas_call | solution.py:360
  (16 shorter events, 0.1 us)
Async XLA Ops:
  1.9 0.7 copy-start.1
  2.6 0.7 copy-start.2
  4.1 25.5 %all-to-all-start = ((f32[16,2,128]{2,1,0:T(2,128)}), f32[16,2,128]{2,1,0:T(2,128)S(1)}, u32[]{:S(2)}, u32[]{:S(2)}) async-start(f32[16,2,128]{2,1,0:T(2,128)} %get-tuple-element.9), calls=%async_computation | async-start | bytes 32768 | tf_op jit(solution)/shard_map/all_to_all | solution.py:268
  30.4 13.6 %copy-start = (f32[121,512]{1,0:T(8,128)S(1)}, f32[121,512]{1,0:T(8,128)}, u32[]{:S(2)}) copy-start(f32[121,512]{1,0:T(8,128)} %cells_ref.3) | copy-start | bytes 743428
  30.4 26.4 %all-to-all-start.1 = ((f32[64,8,128]{2,1,0:T(8,128)}), f32[64,8,128]{2,1,0:T(8,128)S(1)}, u32[]{:S(2)}, u32[]{:S(2)}) async-start(f32[64,8,128]{2,1,0:T(8,128)} %broadcast_in_dim.9), calls=%async_computation.1 | async-start | bytes 524288 | tf_op jit(solution)/shard_map/all_to_all | solution.py:274
  48.5 20.3 %copy-start.10 = (s32[1,512]{1,0:T(1,128)S(1)}, s32[1,512]{1,0:T(1,128)}, u32[]{:S(2)}) copy-start(s32[1,512]{1,0:T(1,128)} %param.18) | copy-start | bytes 6148
  48.5 20.3 %copy-start.8 = (s32[1,16,64]{2,1,0:T(8,128)S(1)}, s32[1,16,64]{2,1,0:T(8,128)}, u32[]{:S(2)}) copy-start(s32[1,16,64]{2,1,0:T(8,128)} %param.19) | copy-start | bytes 12292
  48.5 20.4 %copy-start.9 = (s32[1,16,64]{2,1,0:T(8,128)S(1)}, s32[1,16,64]{2,1,0:T(8,128)}, u32[]{:S(2)}) copy-start(s32[1,16,64]{2,1,0:T(8,128)} %param.20) | copy-start | bytes 12292
  48.5 20.5 %copy-start.6 = (f32[8,121,121]{2,0,1:T(8,128)S(1)}, f32[8,121,121]{2,0,1:T(8,128)}, u32[]{:S(2)}) copy-start(f32[8,121,121]{2,0,1:T(8,128)} %param.15) | copy-start | bytes 1405540
  56.8 0.7 copy-start.4
  57.5 34.3 %all-to-all-start.2 = ((f32[16,128,128]{2,1,0:T(8,128)}), f32[16,128,128]{2,1,0:T(8,128)S(1)}, u32[]{:S(2)}, u32[]{:S(2)}) async-start(f32[16,128,128]{2,1,0:T(8,128)} %answers.1), calls=%async_computation.2 | async-start | bytes 2097152 | tf_op jit(solution)/shard_map/all_to_all | solution.py:314
  63.8 5.4 %copy-start.7 = (f32[121,121]{1,0:T(8,128)S(1)}, f32[121,121]{1,0:T(8,128)}, u32[]{:S(2)}) copy-start(f32[121,121]{1,0:T(8,128)} %param.16) | copy-start | bytes 175696
  64.5 4.7 %collective-permute-start = (f32[121,16]{1,0:T(8,128)}, f32[121,16]{1,0:T(8,128)}, u32[]{:S(2)}, u32[]{:S(2)}) collective-permute-start(f32[121,16]{1,0:T(8,128)} %get-tuple-element.15), channel_id=1, source_target_pairs={{0,16},{16,32},{32,48},{48,64},{64,80},{80,96},{96,112},{112,128},... | collective-permute-start | bytes 23240 | tf_op jit(solution)/shard_map/ppermute | solution.py:280
  67.5 5.3 %collective-permute-start.1 = (f32[121,16]{1,0:T(8,128)S(1)}, f32[121,16]{1,0:T(8,128)}, u32[]{:S(2)}, u32[]{:S(2)}) collective-permute-start(f32[121,16]{1,0:T(8,128)S(1)} %get-tuple-element.16), channel_id=1, source_target_pairs={{16,0},{32,16},{48,32},{64,48},{80,64},{96,80},{112,96},{128,112},... | collective-permute-start | bytes 23240 | tf_op jit(solution)/shard_map/ppermute | solution.py:281
  73.9 3.2 %copy-start.5 = (f32[64,8,128]{2,1,0:T(8,128)S(1)}, f32[64,8,128]{2,1,0:T(8,128)}, u32[]{:S(2)}) copy-start(f32[64,8,128]{2,1,0:T(8,128)} %copy-done.4) | copy-start | bytes 786436
  73.9 6.4 %copy-start.3 = (f32[64,1024]{1,0:T(8,128)S(1)}, f32[64,1024]{1,0:T(8,128)}, u32[]{:S(2)}) copy-start(f32[64,1024]{1,0:T(8,128)} %weight_ref.1) | copy-start | bytes 786436

commit v4 on v3

--- a/solution.py
+++ b/solution.py
@@ -190,36 +190,15 @@
     out_ref[...] = jnp.concatenate([pack_ids(their_ref[...]), pack_ids(own_ref[...])], axis=1)
 
 
-def spread_ids(ids, counts):
-    peers, offsets, room = ids.shape
-    slots = offsets * room
-    value = ids.reshape(peers * offsets, room).astype(F32)
-    high = jnp.floor(value * (1.0 / 32.0))
-    both = jnp.concatenate([high, value - 32.0 * high], axis=0).astype(BF16)
-    row = lax.broadcasted_iota(jnp.int32, (room, slots), 0)
-    lane = lax.broadcasted_iota(jnp.int32, (room, slots), 1)
-    wide = dot(both, jnp.where(lane % room == row, 1.0, 0.0).astype(BF16), NN)
-    wide = 32.0 * wide[: peers * offsets] + wide[peers * offsets :]
-    wide = wide.reshape(peers, offsets, slots)
-    row = lax.broadcasted_iota(jnp.int32, wide.shape, 1)
-    lane = lax.broadcasted_iota(jnp.int32, wide.shape, 2)
-    flat = jnp.sum(jnp.where(lane // room == row, wide, 0.0), axis=1)
-    row = lax.broadcasted_iota(jnp.int32, (offsets, slots), 0)
-    lane = lax.broadcasted_iota(jnp.int32, (offsets, slots), 1)
-    count = dot(counts.astype(F32).astype(BF16), jnp.where(lane // room == row, 1.0, 0.0).astype(BF16), NN)
-    slot = lax.broadcasted_iota(jnp.int32, flat.shape, 1) % room
-    return jnp.where(slot.astype(F32) < count, flat, -1.0)
-
-
-def message_kernel(source_ref, target_ref, count_ref, top_ref, out_ref, own_source_ref):
-    peers = target_ref.shape[0]
+def message_kernel(target_ref, count_ref, top_ref, out_ref):
+    peers, room, offsets = target_ref.shape
+    coefs = top_ref.shape[1]
     counts = count_ref[...]
-    coefs = top_ref.shape[1]
-    own_source_ref[...] = spread_ids(source_ref[...], counts)
-    own_target = spread_ids(target_ref[...], counts)
+    for c in range(room):
+        ids = jnp.where(c < counts, target_ref[:, c, :], -1).astype(F32)
+        out_ref[:, 0, c * offsets : (c + 1) * offsets] = ids
     out_ref[:, 1, :coefs] = jnp.broadcast_to(top_ref[...], (peers, coefs))
     out_ref[:, 1, coefs:] = jnp.zeros((peers, WIDE - coefs), F32)
-    out_ref[:, 0, :] = own_target
 
 
 def sum_kernel(terms_ref, target_ref, near_ref, out_ref, total):
@@ -256,38 +235,23 @@
     segs = lax.axis_size("seg")
     params = pltpu.CompilerParams(vmem_limit_bytes=48 * 1024 * 1024)
 
-    message, own_source = pl.pallas_call(
+    message = pl.pallas_call(
         message_kernel,
-        out_shape=(
-            jax.ShapeDtypeStruct((peers, 2, WIDE), F32),
-            jax.ShapeDtypeStruct((peers, slots), F32),
-        ),
-        compiler_params=params,
+        out_shape=jax.ShapeDtypeStruct((peers, 2, WIDE), F32),
         name="message",
-    )(pair_sources[0], peer_target_cells[0], pair_counts[0], top_multipoles.reshape(1, coefs))
+    )(peer_target_cells[0].transpose(0, 2, 1), pair_counts[0], top_multipoles.reshape(1, coefs))
     arrived = lax.all_to_all(message, "sub", split_axis=0, concat_axis=0, tiled=True)
-    their_target, tops = arrived[:, 0], arrived[:, 1]
-
-    core = lax.axis_index("sub") % 2
-    half = peers // 2
-    mine = lax.dynamic_slice_in_dim(tops, core * half, half, axis=0)
-    spread = lax.all_to_all(
-        jnp.broadcast_to(mine[None], (segs, half, WIDE)), "seg", split_axis=0, concat_axis=0, tiled=True
-    )
-
-    up = [(i, i + 1) for i in range(segs - 1)]
-    down = [(j, i) for i, j in up]
-    before = lax.ppermute(multipoles[:, cells - HALO :], "seg", up)
-    after = lax.ppermute(multipoles[:, :HALO], "seg", down)
-    window = jnp.concatenate([before, multipoles, after], axis=1)
-    span = cells + WIDE
-    window = jnp.pad(window, ((0, pad), (0, span - window.shape[1])))
-
+    their_target, tops = arrived[:, 0].reshape(peers, room, offsets), arrived[:, 1]
+
+    def by_peer(ids):
+        return ids.transpose(0, 2, 1).reshape(peers, slots).astype(F32)
+
+    def by_offset(ids):
+        return ids.transpose(2, 0, 1).reshape(offsets, -1).astype(F32)
+
+    used = lax.broadcasted_iota(jnp.int32, (peers, room, offsets), 1) < pair_counts[0][:, None, :]
+    own_source = jnp.where(used, pair_sources[0].transpose(0, 2, 1), -1)
     operators = three_terms(translators)
-
-    def by_offset(ids):
-        return ids.reshape(peers, offsets, room).transpose(1, 0, 2).reshape(offsets, -1)
-
     scratch = [
         pltpu.VMEM((WIDE, cells), F32),
         pltpu.VMEM((offsets * peers * room, WIDE), F32),
@@ -301,7 +265,24 @@
         compiler_params=params,
         cost_estimate=pair_cost,
         name="listed_terms",
-    )(multipoles, by_offset(own_source), own_source, operators)
+    )(multipoles, by_offset(own_source), by_peer(own_source), operators)
+    tops, listed = lax.optimization_barrier((tops, listed))
+
+    core = lax.axis_index("sub") % 2
+    half = peers // 2
+    mine = lax.dynamic_slice_in_dim(tops, core * half, half, axis=0)
+    spread = lax.all_to_all(
+        jnp.broadcast_to(mine[None], (segs, half, WIDE)), "seg", split_axis=0, concat_axis=0, tiled=True
+    )
+
+    up = [(i, i + 1) for i in range(segs - 1)]
+    down = [(j, i) for i, j in up]
+    before = lax.ppermute(multipoles[:, cells - HALO :], "seg", up)
+    after = lax.ppermute(multipoles[:, :HALO], "seg", down)
+    window = jnp.concatenate([before, multipoles, after], axis=1)
+    span = cells + WIDE
+    window = jnp.pad(window, ((0, pad), (0, span - window.shape[1])))
+
     packet = pl.pallas_call(
         answer_kernel,
         out_shape=jax.ShapeDtypeStruct((peers, 2 * PACK, WIDE), F32),
@@ -309,7 +290,7 @@
         compiler_params=params,
         cost_estimate=pair_cost,
         name="answers",
-    )(multipoles, by_offset(their_target), their_target, operators, listed)
+    )(multipoles, by_offset(their_target), by_peer(their_target), operators, listed)
     packet, spread = lax.optimization_barrier((packet, spread))
     received = lax.all_to_all(packet, "sub", split_axis=0, concat_axis=0, tiled=True)
     every_top = lax.all_gather(
@@ -324,7 +305,7 @@
         out_shape=jax.ShapeDtypeStruct((peers, 2 * PACK), F32),
         compiler_params=params,
         name="packed_targets",
-    )(their_target, own_source)
+    )(by_peer(their_target), by_peer(own_source))
 
     shifts = jnp.pad(child_shifts, ((0, 0), (0, pad), (0, pad)))
     far = jnp.pad(far_operator, ((0, pad), (0, pad)))

time: 93.9 us -> 92.2 us (0.982)
  local copies, waits for them, and re-layouts: 7.79 us -> 5.79 us
    all_to_all x1, waiting for transfers between devices: 5.26 us -> 1.8 us  [body(): lax.all_to_all(message, 'sub', split_axis=0, concat_axis=0, tiled=True)]
    all_to_all x1, waiting for transfers between devices: 9.4 us -> 11.7 us  [body(): lax.all_to_all(packet, 'sub', split_axis=0, concat_axis=0, tiled=True)]
    unnamed x26 -> x19, local copies, waits for them, and re-layouts: 5.65 us -> 3.43 us
    all_to_all x1, waiting for transfers between devices: 8.24 us -> 10.1 us  [body(): lax.all_to_all(jnp.broadcast_to(mine[None], (segs, half, WIDE)), 'seg', s...]
    all_to_all x1, starting transfers between devices: 6.34 us -> 7.96 us  [body(): lax.all_to_all(packet, 'sub', split_axis=0, concat_axis=0, tiled=True)]
    ppermute x1, waiting for transfers between devices: 3.61 us -> 2.58 us  [body(): after = lax.ppermute(multipoles[:, :HALO], 'seg', down)]
  transfers between devices with their start and end apart: 5 -> 5, of which waited for: 4 -> 4; matrix products, arithmetic and copies ran while one was open for 5% -> 6% of each run, Pallas kernels for 10% -> 10%
where the time goes in v4:
time: 92.2 us; the launch traced here: 91.6 us
  starting transfers between devices  43.1 us (47%)
  waiting for transfers between devices  26.2 us (28%)
  Pallas kernels  12.5 us (14%)
  local copies, waits for them, and re-layouts  5.79 us (6%)
  blocking collectives  3.01 us (3%)
    all_to_all x1, starting transfers between devices, body(): lax.all_to_all(message, 'sub', split_axis=0, concat_axis=0, tiled=True)  18.2 us
    all_to_all x1, starting transfers between devices, body(): lax.all_to_all(jnp.broadcast_to(mine[None], (segs, half, WIDE)), 'seg', s...  13.2 us
    all_to_all x1, waiting for transfers between devices, body(): lax.all_to_all(packet, 'sub', split_axis=0, concat_axis=0, tiled=True)  11.7 us
    all_to_all x1, waiting for transfers between devices, body(): lax.all_to_all(jnp.broadcast_to(mine[None], (segs, half, WIDE)), 'seg', s...  10.1 us
    all_to_all x1, starting transfers between devices, body(): lax.all_to_all(packet, 'sub', split_axis=0, concat_axis=0, tiled=True)  7.96 us
    unnamed x19, local copies, waits for them, and re-layouts  3.43 us
    all_gather x1, blocking collectives, body(): lax.all_gather(spread, 'sub', axis=0, tiled=False, axis_index_groups=[[2...  3.01 us
    pallas_call x1, Pallas kernels, body(): pl.pallas_call(answer_kernel, out_shape=jax.ShapeDtypeStruct((peers, 2 *...  2.6 us
  transfers between devices with their start and end apart: 5, of which 4 were waited for; matrix products, arithmetic and copies ran while one was open for 6% of the time, Pallas kernels for 10%

profile of v4, /device:TPU:1, one launch (start us, length us, event | category | flops | bytes accessed | tf_op | source)
XLA Modules:
  0.0 91.6 jit_solution(8866705473235840490)
XLA Ops:
  0.0 1.7 %message.1 = f32[16,2,128]{2,1,0:T(2,128)} custom-call(s32[16,8,16]{2,1,0:T(8,128)} %bitcast.37, s32[16,16]{1,0:T(8,128)} %bitcast.34, f32[1,121]{1,0:T(1,128)} %bitcast.39), custom_call_target="tpu_custom_call" | custom-call | tf_op jit(solution)/shard_map/message/pallas_call | solution.py:238
  1.7 18.2 %all-to-all-start = ((f32[16,2,128]{2,1,0:T(2,128)}), f32[16,2,128]{2,1,0:T(2,128)S(1)}, u32[]{:S(2)}, u32[]{:S(2)}) async-start(f32[16,2,128]{2,1,0:T(2,128)} %message.1), calls=%async_computation | async-start | bytes 32768 | tf_op jit(solution)/shard_map/all_to_all | solution.py:243
  19.9 0.8 copy.32
  20.6 1.6 %copy.31 = f32[16,121,121]{1,2,0:T(8,128)S(1)} copy(f32[16,121,121]{2,0,1:T(8,128)} %param.14) | data formatting | bytes 1874048 | tf_op args[2]
  22.2 0.0 copy-start.3
  22.3 0.2 reduce-precision_convert_fusion
  22.5 0.0 copy-start
  22.5 0.1 copy.33
  22.5 0.6 copy-done.2
  23.1 0.1 copy.34
  23.2 0.1 copy.35
  23.2 0.1 iota.17
  23.3 0.0 copy-done.3
  23.4 0.1 copy.36.by_offset_ref
  23.4 0.3 pad_maximum_fusion.operator_ref
  23.8 0.0 copy-done
  23.8 1.6 %listed_terms.1.listed_ref = f32[16,64,128]{2,1,0:T(8,128)S(1)} custom-call(f32[121,512]{1,0:T(8,128)S(1)} %copy-done, f32[16,128]{1,0:T(8,128)S(1)} %copy.36.by_offset_ref, f32[16,128]{1,0:T(8,128)S(1)} %select_convert_fusion.ids_ref.own_ref, bf16[16,384,128]{2,1,0:T(8,128)(2,1)S(1)} %pad_maximum_fusion.operator_ref), custom_call_target="tpu_custom_call" | custom-call | flops 2000000000 | bytes 3000000 | tf_op jit(solution)/shard_map/listed_terms/pallas_call | solution.py:261
  25.4 1.8 %all-to-all-done = f32[16,2,128]{2,1,0:T(2,128)S(1)} async-done(((f32[16,2,128]{2,1,0:T(2,128)}), f32[16,2,128]{2,1,0:T(2,128)S(1)}, u32[]{:S(2)}, u32[]{:S(2)}) %all-to-all-start) | async-done | bytes 16416 | tf_op jit(solution)/shard_map/all_to_all | solution.py:243
  27.2 0.7 broadcast_in_dim.14
  28.0 13.2 %all-to-all-start.1 = ((f32[64,8,128]{2,1,0:T(8,128)}), f32[64,8,128]{2,1,0:T(8,128)S(1)}, u32[]{:S(2)}, u32[]{:S(2)}) async-start(f32[64,8,128]{2,1,0:T(8,128)} %broadcast_in_dim.14), calls=%async_computation.1 | async-start | bytes 524288 | tf_op jit(solution)/shard_map/all_to_all | solution.py:274
  41.2 0.1 reshape_squeeze.2
  41.3 0.1 copy.30
  41.4 0.1 copy.38.ids_ref.their_ref
  41.4 0.1 copy.37.by_offset_ref
  41.5 2.6 %answers.1 = f32[16,128,128]{2,1,0:T(8,128)} custom-call(f32[121,512]{1,0:T(8,128)S(1)} %copy-done, f32[16,128]{1,0:T(8,128)S(1)} %copy.37.by_offset_ref, f32[16,128]{1,0:T(8,128)S(1)} %copy.38.ids_ref.their_ref, bf16[16,384,128]{2,1,0:T(8,128)(2,1)S(1)} %pad_maximum_fusion.operator_ref, f32[16,64,128]{2,1,0:T(8,128)S(1)} %listed_terms.1.listed_ref), custom_call_target="tpu_custom_call" | custom-call | flops 2000000000 | bytes 3000000 | tf_op jit(solution)/shard_map/answers/pallas_call | solution.py:286
  44.1 10.1 %all-to-all-done.1 = f32[64,8,128]{2,1,0:T(8,128)S(1)} async-done(((f32[64,8,128]{2,1,0:T(8,128)}), f32[64,8,128]{2,1,0:T(8,128)S(1)}, u32[]{:S(2)}, u32[]{:S(2)}) %all-to-all-start.1) | async-done | bytes 262176 | tf_op jit(solution)/shard_map/all_to_all | solution.py:274
  54.2 8.0 %all-to-all-start.2 = ((f32[16,128,128]{2,1,0:T(8,128)}), f32[16,128,128]{2,1,0:T(8,128)S(1)}, u32[]{:S(2)}, u32[]{:S(2)}) async-start(f32[16,128,128]{2,1,0:T(8,128)} %answers.1), calls=%async_computation.2 | async-start | bytes 2097152 | tf_op jit(solution)/shard_map/all_to_all | solution.py:295
  62.2 0.1 fusion.6
  62.3 2.4 %collective-permute-start = (f32[121,16]{1,0:T(8,128)S(1)}, f32[121,16]{1,0:T(8,128)S(1)}, u32[]{:S(2)}, u32[]{:S(2)}) collective-permute-start(f32[121,16]{1,0:T(8,128)S(1)} %get-tuple-element.15), channel_id=1, source_target_pairs={{0,16},{16,32},{32,48},{48,64},{64,80},{80,96},{96,112},{112,128},... | collective-permute-start | bytes 23240 | tf_op jit(solution)/shard_map/ppermute | solution.py:280
  64.7 1.3 %collective-permute-start.1 = (f32[121,16]{1,0:T(8,128)S(1)}, f32[121,16]{1,0:T(8,128)S(1)}, u32[]{:S(2)}, u32[]{:S(2)}) collective-permute-start(f32[121,16]{1,0:T(8,128)S(1)} %get-tuple-element.16), channel_id=1, source_target_pairs={{16,0},{32,16},{48,32},{64,48},{80,64},{96,80},{112,96},{128,112},... | collective-permute-start | bytes 23240 | tf_op jit(solution)/shard_map/ppermute | solution.py:281
  66.0 0.0 copy-done.7
  66.0 0.0 copy-done.5
  66.0 0.1 convert_element_type.36.source_ref
  66.1 0.0 copy-done.6
  66.1 0.1 convert_element_type.38.target_ref
  66.2 1.1 %copy.40 = f32[8,121,121]{2,1,0:T(8,128)S(1)} copy(f32[8,121,121]{2,0,1:T(8,128)} %param.15) | data formatting | bytes 937024 | tf_op args[3]
  67.4 0.0 copy-done.4
  67.4 0.0 collective-permute-done
  67.4 2.6 %collective-permute-done.1 = f32[121,16]{1,0:T(8,128)S(1)} collective-permute-done((f32[121,16]{1,0:T(8,128)S(1)}, f32[121,16]{1,0:T(8,128)S(1)}, u32[]{:S(2)}, u32[]{:S(2)}) %collective-permute-start.1) | collective-permute-done | bytes 7776 | tf_op jit(solution)/shard_map/ppermute | solution.py:281
  70.0 0.2 select_maximum_fusion.window_ref
  70.2 0.0 copy-start.1
  70.2 2.4 %inner_pairs.1.near_ref = f32[512,128]{1,0:T(8,128)S(1)} custom-call(f32[128,640]{1,0:T(8,128)S(1)} %select_maximum_fusion.window_ref, f32[8,128]{1,0:T(8,128)S(1)} %convert_element_type.36.source_ref, f32[8,128]{1,0:T(8,128)S(1)} %convert_element_type.38.target_ref, bf16[16,384,128]{2,1,0:T(8,128)(2,1)S(1)} %pad_maximum_fusion.operator_ref), custom_call_target="tpu_custom_call" | custom-call | flops 2000000000 | bytes 3000000 | tf_op jit(solution)/shard_map/inner_pairs/pallas_call | solution.py:314
  72.6 0.7 packed_targets.1.target_ref
  73.3 3.0 %all-gather = f32[128,8,128]{2,1,0:T(8,128)S(1)} all-gather(f32[64,8,128]{2,1,0:T(8,128)S(1)} %all-to-all-done.1), channel_id=2, replica_groups={{0,1},{2,3},{4,5},{6,7},{8,9},{10,11},{12,13},{14,15},{16,17},{18,19},{..., dimensions={0}, use_global_device_ids=true | all-gather | bytes 786432 | tf_op jit(solution)/shard_map/all_gather | solution.py:296
  76.3 0.0 copy-done.1
  76.3 2.1 %far_field.1.near_ref = f32[512,128]{1,0:T(8,128)S(1)} custom-call(f32[2,64,8,128]{3,2,1,0:T(8,128)S(1)} %bitcast.29, f32[64,1024]{1,0:T(8,128)S(1)} %copy-done.1, f32[128,128]{1,0:T(8,128)S(1)} %pad.17.far_ref, f32[8,128,128]{2,1,0:T(8,128)S(1)} %pad.18.shift_ref, f32[1,512]{1,0:T(1,128)S(1)} %fusion.5.place_ref, f32[512,128]{1,0:T(8,128)S(1)} %inner_pairs.1.near_ref), custom_call_target="tpu_custom_call" | custom-call | flops 1000000000 | bytes 2000000 | tf_op jit(solution)/shard_map/far_field/pallas_call | solution.py:333
  78.4 11.7 %all-to-all-done.2.terms_ref = f32[16,128,128]{2,1,0:T(8,128)S(1)} async-done(((f32[16,128,128]{2,1,0:T(8,128)}), f32[16,128,128]{2,1,0:T(8,128)S(1)}, u32[]{:S(2)}, u32[]{:S(2)}) %all-to-all-start.2) | async-done | bytes 1048608 | tf_op jit(solution)/shard_map/all_to_all | solution.py:295
  90.1 1.5 %sum_terms.1 = f32[121,512]{1,0:T(8,128)} custom-call(f32[16,128,128]{2,1,0:T(8,128)S(1)} %all-to-all-done.2.terms_ref, f32[16,128]{1,0:T(8,128)S(1)} %packed_targets.1.target_ref, f32[512,128]{1,0:T(8,128)S(1)} %far_field.1.near_ref), custom_call_target="tpu_custom_call" | custom-call | flops 2000000000 | bytes 3000000 | tf_op jit(solution)/shard_map/sum_terms/pallas_call | solution.py:341
  (16 shorter events, 0.2 us)
Async XLA Ops:
  1.7 25.5 %all-to-all-start = ((f32[16,2,128]{2,1,0:T(2,128)}), f32[16,2,128]{2,1,0:T(2,128)S(1)}, u32[]{:S(2)}, u32[]{:S(2)}) async-start(f32[16,2,128]{2,1,0:T(2,128)} %message.1), calls=%async_computation | async-start | bytes 32768 | tf_op jit(solution)/shard_map/all_to_all | solution.py:243
  22.2 0.8 copy-start.2
  22.2 1.1 %copy-start.3 = (s32[1,16,16]{2,1,0:T(8,128)S(1)}, s32[1,16,16]{2,1,0:T(8,128)}, u32[]{:S(2)}) copy-start(s32[1,16,16]{2,1,0:T(8,128)} %param.23) | copy-start | bytes 3076
  22.5 1.3 %copy-start = (f32[121,512]{1,0:T(8,128)S(1)}, f32[121,512]{1,0:T(8,128)}, u32[]{:S(2)}) copy-start(f32[121,512]{1,0:T(8,128)} %cells_ref.3) | copy-start | bytes 743428
  28.0 26.2 %all-to-all-start.1 = ((f32[64,8,128]{2,1,0:T(8,128)}), f32[64,8,128]{2,1,0:T(8,128)S(1)}, u32[]{:S(2)}, u32[]{:S(2)}) async-start(f32[64,8,128]{2,1,0:T(8,128)} %broadcast_in_dim.14), calls=%async_computation.1 | async-start | bytes 524288 | tf_op jit(solution)/shard_map/all_to_all | solution.py:274
  44.1 21.9 %copy-start.7 = (s32[1,512]{1,0:T(1,128)S(1)}, s32[1,512]{1,0:T(1,128)}, u32[]{:S(2)}) copy-start(s32[1,512]{1,0:T(1,128)} %param.18) | copy-start | bytes 6148
  44.1 21.9 %copy-start.5 = (s32[1,16,64]{2,1,0:T(8,128)S(1)}, s32[1,16,64]{2,1,0:T(8,128)}, u32[]{:S(2)}) copy-start(s32[1,16,64]{2,1,0:T(8,128)} %param.19) | copy-start | bytes 12292
  44.1 22.0 %copy-start.6 = (s32[1,16,64]{2,1,0:T(8,128)S(1)}, s32[1,16,64]{2,1,0:T(8,128)}, u32[]{:S(2)}) copy-start(s32[1,16,64]{2,1,0:T(8,128)} %param.20) | copy-start | bytes 12292
  54.2 35.9 %all-to-all-start.2 = ((f32[16,128,128]{2,1,0:T(8,128)}), f32[16,128,128]{2,1,0:T(8,128)S(1)}, u32[]{:S(2)}, u32[]{:S(2)}) async-start(f32[16,128,128]{2,1,0:T(8,128)} %answers.1), calls=%async_computation.2 | async-start | bytes 2097152 | tf_op jit(solution)/shard_map/all_to_all | solution.py:295
  62.2 5.2 %copy-start.4 = (f32[121,121]{1,0:T(8,128)S(1)}, f32[121,121]{1,0:T(8,128)}, u32[]{:S(2)}) copy-start(f32[121,121]{1,0:T(8,128)} %param.16) | copy-start | bytes 175696
  62.3 5.1 %collective-permute-start = (f32[121,16]{1,0:T(8,128)S(1)}, f32[121,16]{1,0:T(8,128)S(1)}, u32[]{:S(2)}, u32[]{:S(2)}) collective-permute-start(f32[121,16]{1,0:T(8,128)S(1)} %get-tuple-element.15), channel_id=1, source_target_pairs={{0,16},{16,32},{32,48},{48,64},{64,80},{80,96},{96,112},{112,128},... | collective-permute-start | bytes 23240 | tf_op jit(solution)/shard_map/ppermute | solution.py:280
  64.7 5.3 %collective-permute-start.1 = (f32[121,16]{1,0:T(8,128)S(1)}, f32[121,16]{1,0:T(8,128)S(1)}, u32[]{:S(2)}, u32[]{:S(2)}) collective-permute-start(f32[121,16]{1,0:T(8,128)S(1)} %get-tuple-element.16), channel_id=1, source_target_pairs={{16,0},{32,16},{48,32},{64,48},{80,64},{96,80},{112,96},{128,112},... | collective-permute-start | bytes 23240 | tf_op jit(solution)/shard_map/ppermute | solution.py:281
  70.2 6.2 %copy-start.1 = (f32[64,1024]{1,0:T(8,128)S(1)}, f32[64,1024]{1,0:T(8,128)}, u32[]{:S(2)}) copy-start(f32[64,1024]{1,0:T(8,128)} %weight_ref.1) | copy-start | bytes 786436

commit v5 on v4

--- a/solution.py
+++ b/solution.py
@@ -102,9 +102,14 @@
     out_ref[...] = halves(total[...])
 
 
-def far_kernel(top_ref, weight_ref, far_ref, shift_ref, place_ref, near_ref, out_ref):
-    top = jnp.concatenate([top_ref[0][:, None], top_ref[1][:, None]], axis=1)
-    top = top.reshape(-1, WIDE)
+def far_kernel(place_x_ref, top_ref, weight_ref, far_ref, shift_ref, place_ref, near_ref, out_ref):
+    xs = top_ref.shape[1]
+    top = []
+    for x in range(xs):
+        ahead = lax.rem(x + place_x_ref[0], min(xs, 2)) * (xs // 2) + x // 2
+        both = [top_ref[core, ahead][:, None] for core in (0, 1)]
+        top.append(jnp.concatenate(both, axis=1).reshape(-1, WIDE))
+    top = jnp.concatenate(top, axis=0)
     summed = dot_exact(weight_ref[...], top, NN)
     parent = dot_exact(summed, far_ref[...], NT)
     table = jnp.concatenate(
@@ -213,6 +218,13 @@
     out_ref[...] = jnp.transpose(result)[:coefs, :]
 
 
+def grid(segs):
+    ys = 1
+    while ys * ys < segs:
+        ys *= 2
+    return segs // ys, ys
+
+
 def body(
     multipoles,
     top_multipoles,
@@ -268,20 +280,19 @@
     )(multipoles, by_offset(own_source), by_peer(own_source), operators)
     tops, listed = lax.optimization_barrier((tops, listed))
 
+    xs, ys = grid(segs)
     core = lax.axis_index("sub") % 2
     half = peers // 2
     mine = lax.dynamic_slice_in_dim(tops, core * half, half, axis=0)
     spread = lax.all_to_all(
-        jnp.broadcast_to(mine[None], (segs, half, WIDE)), "seg", split_axis=0, concat_axis=0, tiled=True
-    )
-
-    up = [(i, i + 1) for i in range(segs - 1)]
-    down = [(j, i) for i, j in up]
-    before = lax.ppermute(multipoles[:, cells - HALO :], "seg", up)
-    after = lax.ppermute(multipoles[:, :HALO], "seg", down)
-    window = jnp.concatenate([before, multipoles, after], axis=1)
-    span = cells + WIDE
-    window = jnp.pad(window, ((0, pad), (0, span - window.shape[1])))
+        jnp.broadcast_to(mine[None], (max(xs // 2, 1) * ys, half, WIDE)),
+        "seg",
+        split_axis=0,
+        concat_axis=0,
+        tiled=True,
+        axis_index_groups=[[x * ys + y for x in range(odd, xs, 2) for y in range(ys)] for odd in range(min(xs, 2))],
+    )
+
 
     packet = pl.pallas_call(
         answer_kernel,
@@ -293,13 +304,29 @@
     )(multipoles, by_offset(their_target), by_peer(their_target), operators, listed)
     packet, spread = lax.optimization_barrier((packet, spread))
     received = lax.all_to_all(packet, "sub", split_axis=0, concat_axis=0, tiled=True)
+
+    last, first = multipoles[:, cells - HALO :], multipoles[:, :HALO]
+    block = spread.reshape(1, -1, WIDE)
+    if xs > 1:
+        pairs = [(x * ys + y, (x ^ 1) * ys + y) for x in range(xs) for y in range(ys)]
+        block = jnp.concatenate([block, lax.ppermute(block, "seg", pairs)], axis=0)
     every_top = lax.all_gather(
-        spread,
+        block,
         "sub",
         axis=0,
-        tiled=False,
+        tiled=True,
         axis_index_groups=[[2 * i, 2 * i + 1] for i in range(half)],
     )
+    every_top = every_top.reshape(2, xs, ys, half, WIDE)
+    place_x = (lax.axis_index("seg") // ys).astype(jnp.int32).reshape(1)
+    up = [(i, i + 1) for i in range(segs - 1)]
+    down = [(j, i) for i, j in up]
+    before = lax.ppermute(last, "seg", up)
+    after = lax.ppermute(first, "seg", down)
+    window = jnp.concatenate([before, multipoles, after], axis=1)
+    span = cells + WIDE
+    window = jnp.pad(window, ((0, pad), (0, span - window.shape[1])))
+
     targets = pl.pallas_call(
         target_kernel,
         out_shape=jax.ShapeDtypeStruct((peers, 2 * PACK), F32),
@@ -332,11 +359,12 @@
     place = (cell_codes % octants * parents + cell_codes // octants).astype(F32)
     near = pl.pallas_call(
         far_kernel,
+        in_specs=[pl.BlockSpec(memory_space=pltpu.SMEM)] + [pl.BlockSpec(memory_space=pltpu.VMEM)] * 6,
         out_shape=jax.ShapeDtypeStruct((cells, WIDE), F32),
         compiler_params=params,
         cost_estimate=pl.CostEstimate(flops=10**9, bytes_accessed=2 * 10**6, transcendentals=0),
         name="far_field",
-    )(every_top, far_weights, far, shifts, place, near)
+    )(place_x, every_top, far_weights, far, shifts, place, near)
 
     return pl.pallas_call(
         sum_kernel,

time: 92.2 us -> 89.7 us (0.973)
  waiting for transfers between devices: 26.2 us -> 18.9 us
  starting transfers between devices: 43.1 us -> 45 us
  blocking collectives: 3.01 us -> 3.98 us
  other arithmetic: 0.71 us -> 1.67 us
  local copies, waits for them, and re-layouts: 5.79 us -> 6.74 us
    all_to_all x1, waiting for transfers between devices: 11.7 us -> 4.92 us  [body(): lax.all_to_all(packet, 'sub', split_axis=0, concat_axis=0, tiled=True)]
    ppermute x2 -> x3, starting transfers between devices: 3.71 us -> 7.16 us  [the longest x1 3.31 us: body(): before = lax.ppermute(last, 'seg', up)]
    all_to_all x1, waiting for transfers between devices: 10.1 us -> 8.54 us  [body(): lax.all_to_all(jnp.broadcast_to(mine[None], (max(xs // 2, 1) * ys, half,...]
    ppermute x2 -> x3, waiting for transfers between devices: 2.58 us -> 3.61 us  [the longest x1 2.99 us: body(): after = lax.ppermute(first, 'seg', down)]
    all_gather x1, blocking collectives: 3.01 us -> 3.98 us  [body(): lax.all_gather(block, 'sub', axis=0, tiled=True, axis_index_groups=[[2 *...]
    unnamed x19 -> x23, local copies, waits for them, and re-layouts: 3.43 us -> 2.98 us
  transfers between devices with their start and end apart: 5 -> 6, of which waited for: 4 -> 5; matrix products, arithmetic and copies ran while one was open for 6% -> 7% of each run, Pallas kernels for 10% -> 11%
where the time goes in v5:
time: 89.7 us; the launch traced here: 89.1 us
  starting transfers between devices  45 us (50%)
  waiting for transfers between devices  18.9 us (21%)
  Pallas kernels  12.5 us (14%)
  local copies, waits for them, and re-layouts  6.74 us (8%)
  blocking collectives  3.98 us (4%)
  other arithmetic  1.67 us (2%)
    all_to_all x1, starting transfers between devices, body(): lax.all_to_all(message, 'sub', split_axis=0, concat_axis=0, tiled=True)  18.2 us
    all_to_all x1, starting transfers between devices, body(): lax.all_to_all(jnp.broadcast_to(mine[None], (max(xs // 2, 1) * ys, half,...  12.6 us
    all_to_all x1, waiting for transfers between devices, body(): lax.all_to_all(jnp.broadcast_to(mine[None], (max(xs // 2, 1) * ys, half,...  8.54 us
    all_to_all x1, starting transfers between devices, body(): lax.all_to_all(packet, 'sub', split_axis=0, concat_axis=0, tiled=True)  7.06 us
    all_to_all x1, waiting for transfers between devices, body(): lax.all_to_all(packet, 'sub', split_axis=0, concat_axis=0, tiled=True)  4.92 us
    all_gather x1, blocking collectives, body(): lax.all_gather(block, 'sub', axis=0, tiled=True, axis_index_groups=[[2 *...  3.98 us
    ppermute x1, starting transfers between devices, body(): before = lax.ppermute(last, 'seg', up)  3.31 us
    ppermute x1, waiting for transfers between devices, body(): after = lax.ppermute(first, 'seg', down)  2.99 us
  transfers between devices with their start and end apart: 6, of which 5 were waited for; matrix products, arithmetic and copies ran while one was open for 7% of the time, Pallas kernels for 11%

profile of v5, /device:TPU:1, one launch (start us, length us, event | category | flops | bytes accessed | tf_op | source)
XLA Modules:
  0.0 89.1 jit_solution(1303085023183920460)
XLA Ops:
  0.0 1.7 %message.1 = f32[16,2,128]{2,1,0:T(2,128)} custom-call(s32[16,8,16]{2,1,0:T(8,128)} %bitcast.41, s32[16,16]{1,0:T(8,128)} %bitcast.38, f32[1,121]{1,0:T(1,128)} %bitcast.43), custom_call_target="tpu_custom_call" | custom-call | tf_op jit(solution)/shard_map/message/pallas_call | solution.py:250
  1.7 18.2 %all-to-all-start = ((f32[16,2,128]{2,1,0:T(2,128)}), f32[16,2,128]{2,1,0:T(2,128)S(1)}, u32[]{:S(2)}, u32[]{:S(2)}) async-start(f32[16,2,128]{2,1,0:T(2,128)} %message.1), calls=%async_computation | async-start | bytes 32768 | tf_op jit(solution)/shard_map/all_to_all | solution.py:255
  19.9 0.8 copy.32
  20.6 1.6 %copy.31 = f32[16,121,121]{1,2,0:T(8,128)S(1)} copy(f32[16,121,121]{2,0,1:T(8,128)} %param.14) | data formatting | bytes 1874048 | tf_op args[2]
  22.2 0.0 copy-start.6
  22.3 0.3 reduce-precision_convert_fusion
  22.5 0.0 copy-start
  22.6 0.1 copy.33
  22.6 0.5 copy-done.5
  23.1 0.1 copy.34
  23.2 0.1 copy.35
  23.2 0.1 iota.17
  23.4 0.1 copy.36.by_offset_ref
  23.4 0.3 pad_maximum_fusion.operator_ref
  23.8 1.6 %listed_terms.1.listed_ref = f32[16,64,128]{2,1,0:T(8,128)S(1)} custom-call(f32[121,512]{1,0:T(8,128)S(1)} %copy-done, f32[16,128]{1,0:T(8,128)S(1)} %copy.36.by_offset_ref, f32[16,128]{1,0:T(8,128)S(1)} %select_convert_fusion.ids_ref.own_ref, bf16[16,384,128]{2,1,0:T(8,128)(2,1)S(1)} %pad_maximum_fusion.operator_ref), custom_call_target="tpu_custom_call" | custom-call | flops 2000000000 | bytes 3000000 | tf_op jit(solution)/shard_map/listed_terms/pallas_call | solution.py:273
  25.4 1.8 %all-to-all-done = f32[16,2,128]{2,1,0:T(2,128)S(1)} async-done(((f32[16,2,128]{2,1,0:T(2,128)}), f32[16,2,128]{2,1,0:T(2,128)S(1)}, u32[]{:S(2)}, u32[]{:S(2)}) %all-to-all-start) | async-done | bytes 16416 | tf_op jit(solution)/shard_map/all_to_all | solution.py:255
  27.2 0.7 broadcast_in_dim.14
  27.9 12.6 %all-to-all-start.1 = ((f32[32,8,128]{2,1,0:T(8,128)}), f32[32,8,128]{2,1,0:T(8,128)S(1)}, u32[]{:S(2)}, u32[]{:S(2)}) async-start(f32[32,8,128]{2,1,0:T(8,128)} %broadcast_in_dim.14), calls=%async_computation.1 | async-start | bytes 262144 | tf_op jit(solution)/shard_map/all_to_all | solution.py:287
  40.5 0.1 reshape_squeeze.2
  40.6 0.1 copy.30
  40.7 0.1 copy.38.ids_ref.their_ref
  40.7 0.1 copy.37.by_offset_ref
  40.8 2.6 %answers.1 = f32[16,128,128]{2,1,0:T(8,128)} custom-call(f32[121,512]{1,0:T(8,128)S(1)} %copy-done, f32[16,128]{1,0:T(8,128)S(1)} %copy.37.by_offset_ref, f32[16,128]{1,0:T(8,128)S(1)} %copy.38.ids_ref.their_ref, bf16[16,384,128]{2,1,0:T(8,128)(2,1)S(1)} %pad_maximum_fusion.operator_ref, f32[16,64,128]{2,1,0:T(8,128)S(1)} %listed_terms.1.listed_ref), custom_call_target="tpu_custom_call" | custom-call | flops 2000000000 | bytes 3000000 | tf_op jit(solution)/shard_map/answers/pallas_call | solution.py:297
  43.4 8.5 %all-to-all-done.1 = f32[32,8,128]{2,1,0:T(8,128)S(1)} async-done(((f32[32,8,128]{2,1,0:T(8,128)}), f32[32,8,128]{2,1,0:T(8,128)S(1)}, u32[]{:S(2)}, u32[]{:S(2)}) %all-to-all-start.1) | async-done | bytes 131104 | tf_op jit(solution)/shard_map/all_to_all | solution.py:287
  52.0 0.7 copy-done.2
  52.6 7.1 %all-to-all-start.2 = ((f32[16,128,128]{2,1,0:T(8,128)}), f32[16,128,128]{2,1,0:T(8,128)S(1)}, u32[]{:S(2)}, u32[]{:S(2)}) async-start(f32[16,128,128]{2,1,0:T(8,128)} %answers.1), calls=%async_computation.2 | async-start | bytes 2097152 | tf_op jit(solution)/shard_map/all_to_all | solution.py:306
  59.7 0.7 fusion.6
  60.4 3.3 %collective-permute-start.1 = (f32[121,16]{1,0:T(8,128)}, f32[121,16]{1,0:T(8,128)}, u32[]{:S(2)}, u32[]{:S(2)}) collective-permute-start(f32[121,16]{1,0:T(8,128)} %get-tuple-element.15), channel_id=1, source_target_pairs={{0,16},{16,32},{32,48},{48,64},{64,80},{80,96},{96,112},{112,128},... | collective-permute-start | bytes 23240 | tf_op jit(solution)/shard_map/ppermute | solution.py:324
  63.7 1.3 %collective-permute-start.2 = (f32[121,16]{1,0:T(8,128)}, f32[121,16]{1,0:T(8,128)}, u32[]{:S(2)}, u32[]{:S(2)}) collective-permute-start(f32[121,16]{1,0:T(8,128)} %get-tuple-element.16), channel_id=1, source_target_pairs={{16,0},{32,16},{48,32},{64,48},{80,64},{96,80},{112,96},{128,112},... | collective-permute-start | bytes 23240 | tf_op jit(solution)/shard_map/ppermute | solution.py:325
  65.0 0.0 copy-done.9
  65.1 0.1 convert_element_type.36.source_ref
  65.1 0.1 convert_element_type.38.target_ref
  65.2 0.0 copy-done.4
  65.2 0.1 copy.40
  65.4 0.8 pad.17.far_ref
  66.2 0.0 collective-permute-done.1
  66.2 3.0 %collective-permute-done.2 = f32[121,16]{1,0:T(8,128)} collective-permute-done((f32[121,16]{1,0:T(8,128)}, f32[121,16]{1,0:T(8,128)}, u32[]{:S(2)}, u32[]{:S(2)}) %collective-permute-start.2) | collective-permute-done | bytes 7776 | tf_op jit(solution)/shard_map/ppermute | solution.py:325
  69.2 1.0 %select_maximum_fusion.window_ref = f32[128,640]{1,0:T(8,128)S(1)} fusion(f32[121,16]{1,0:T(8,128)} %collective-permute-done.2, f32[121,512]{1,0:T(8,128)S(1)} %copy-done, f32[121,16]{1,0:T(8,128)} %collective-permute-done.1), kind=kLoop, calls=%fused_computation.4 | loop fusion | flops 901120 | bytes 590976 | tf_op jit(solution)/shard_map/concatenate | solution.py:326
  70.2 0.0 copy-start.3
  70.3 0.0 copy-start.1
  70.3 2.6 %collective-permute-start = (f32[1,256,128]{2,1,0:T(8,128)}, f32[1,256,128]{2,1,0:T(8,128)S(1)}, u32[]{:S(2)}, u32[]{:S(2)}) collective-permute-start(f32[1,256,128]{2,1,0:T(8,128)} %bitcast.34), channel_id=1, source_target_pairs={{0,128},{16,144},{32,160},{48,176},{64,192},{80,208},{96,224},{112... | collective-permute-start | bytes 393224 | tf_op jit(solution)/shard_map/ppermute | solution.py:312
  72.9 2.4 %inner_pairs.1.near_ref = f32[512,128]{1,0:T(8,128)S(1)} custom-call(f32[128,640]{1,0:T(8,128)S(1)} %select_maximum_fusion.window_ref, f32[8,128]{1,0:T(8,128)S(1)} %convert_element_type.36.source_ref, f32[8,128]{1,0:T(8,128)S(1)} %convert_element_type.38.target_ref, bf16[16,384,128]{2,1,0:T(8,128)(2,1)S(1)} %pad_maximum_fusion.operator_ref), custom_call_target="tpu_custom_call" | custom-call | flops 2000000000 | bytes 3000000 | tf_op jit(solution)/shard_map/inner_pairs/pallas_call | solution.py:341
  75.3 0.7 packed_targets.1.target_ref
  76.0 0.6 collective-permute-done
  76.6 4.0 %all_gather.3 = f32[4,256,128]{2,1,0:T(8,128)S(1)} all-gather(f32[2,256,128]{2,1,0:T(8,128)S(1)} %pad_maximum_fusion.1), channel_id=1, replica_groups={{0,1},{2,3},{4,5},{6,7},{8,9},{10,11},{12,13},{14,15},{16,17},{18,19},{..., dimensions={0}, use_global_device_ids=true | all-gather | bytes 786432 | tf_op jit(solution)/shard_map/all_gather | solution.py:313
  80.6 2.1 %far_field.1.near_ref = f32[512,128]{1,0:T(8,128)S(1)} custom-call(s32[1]{0:T(128)} %bitcast.16.place_x_ref, f32[2,8,8,8,128]{4,3,2,1,0:T(8,128)S(1)} %bitcast.31, f32[64,1024]{1,0:T(8,128)S(1)} %copy-done.1, f32[128,128]{1,0:T(8,128)S(1)} %pad.17.far_ref, f32[8,128,128]{2,1,0:T(8,128)S(1)} %pad.18.shift_ref, f32[1,512]{1,0:T(1,128)S(1)} %fusion.5.place_ref, ...), custom_call_target="tpu_custom_call" | custom-call | flops 1000000000 | bytes 2000000 | tf_op jit(solution)/shard_map/far_field/pallas_call | solution.py:360
  82.7 4.9 %all-to-all-done.2.terms_ref = f32[16,128,128]{2,1,0:T(8,128)S(1)} async-done(((f32[16,128,128]{2,1,0:T(8,128)}), f32[16,128,128]{2,1,0:T(8,128)S(1)}, u32[]{:S(2)}, u32[]{:S(2)}) %all-to-all-start.2) | async-done | bytes 1048608 | tf_op jit(solution)/shard_map/all_to_all | solution.py:306
  87.6 1.5 %sum_terms.1 = f32[121,512]{1,0:T(8,128)} custom-call(f32[16,128,128]{2,1,0:T(8,128)S(1)} %all-to-all-done.2.terms_ref, f32[16,128]{1,0:T(8,128)S(1)} %packed_targets.1.target_ref, f32[512,128]{1,0:T(8,128)S(1)} %far_field.1.near_ref), custom_call_target="tpu_custom_call" | custom-call | flops 2000000000 | bytes 3000000 | tf_op jit(solution)/shard_map/sum_terms/pallas_call | solution.py:369
  (23 shorter events, 0.2 us)
Async XLA Ops:
  1.7 25.5 %all-to-all-start = ((f32[16,2,128]{2,1,0:T(2,128)}), f32[16,2,128]{2,1,0:T(2,128)S(1)}, u32[]{:S(2)}, u32[]{:S(2)}) async-start(f32[16,2,128]{2,1,0:T(2,128)} %message.1), calls=%async_computation | async-start | bytes 32768 | tf_op jit(solution)/shard_map/all_to_all | solution.py:255
  22.2 0.8 copy-start.5
  22.2 1.1 %copy-start.6 = (s32[1,16,16]{2,1,0:T(8,128)S(1)}, s32[1,16,16]{2,1,0:T(8,128)}, u32[]{:S(2)}) copy-start(s32[1,16,16]{2,1,0:T(8,128)} %param.23) | copy-start | bytes 3076
  22.5 1.2 %copy-start = (f32[121,512]{1,0:T(8,128)S(1)}, f32[121,512]{1,0:T(8,128)}, u32[]{:S(2)}) copy-start(f32[121,512]{1,0:T(8,128)} %cells_ref.3) | copy-start | bytes 743428
  27.9 24.1 %all-to-all-start.1 = ((f32[32,8,128]{2,1,0:T(8,128)}), f32[32,8,128]{2,1,0:T(8,128)S(1)}, u32[]{:S(2)}, u32[]{:S(2)}) async-start(f32[32,8,128]{2,1,0:T(8,128)} %broadcast_in_dim.14), calls=%async_computation.1 | async-start | bytes 262144 | tf_op jit(solution)/shard_map/all_to_all | solution.py:287
  43.4 21.6 %copy-start.9 = (s32[1,512]{1,0:T(1,128)S(1)}, s32[1,512]{1,0:T(1,128)}, u32[]{:S(2)}) copy-start(s32[1,512]{1,0:T(1,128)} %param.18) | copy-start | bytes 6148
  43.4 21.6 %copy-start.7 = (s32[1,16,64]{2,1,0:T(8,128)S(1)}, s32[1,16,64]{2,1,0:T(8,128)}, u32[]{:S(2)}) copy-start(s32[1,16,64]{2,1,0:T(8,128)} %param.19) | copy-start | bytes 12292
  43.4 21.7 %copy-start.8 = (s32[1,16,64]{2,1,0:T(8,128)S(1)}, s32[1,16,64]{2,1,0:T(8,128)}, u32[]{:S(2)}) copy-start(s32[1,16,64]{2,1,0:T(8,128)} %param.20) | copy-start | bytes 12292
  43.4 21.8 %copy-start.4 = (f32[8,121,121]{2,0,1:T(8,128)S(1)}, f32[8,121,121]{2,0,1:T(8,128)}, u32[]{:S(2)}) copy-start(f32[8,121,121]{2,0,1:T(8,128)} %param.15) | copy-start | bytes 1405540
  52.0 0.7 copy-start.2
  52.6 35.0 %all-to-all-start.2 = ((f32[16,128,128]{2,1,0:T(8,128)}), f32[16,128,128]{2,1,0:T(8,128)S(1)}, u32[]{:S(2)}, u32[]{:S(2)}) async-start(f32[16,128,128]{2,1,0:T(8,128)} %answers.1), calls=%async_computation.2 | async-start | bytes 2097152 | tf_op jit(solution)/shard_map/all_to_all | solution.py:306
  60.4 5.8 %collective-permute-start.1 = (f32[121,16]{1,0:T(8,128)}, f32[121,16]{1,0:T(8,128)}, u32[]{:S(2)}, u32[]{:S(2)}) collective-permute-start(f32[121,16]{1,0:T(8,128)} %get-tuple-element.15), channel_id=1, source_target_pairs={{0,16},{16,32},{32,48},{48,64},{64,80},{80,96},{96,112},{112,128},... | collective-permute-start | bytes 23240 | tf_op jit(solution)/shard_map/ppermute | solution.py:324
  63.7 5.5 %collective-permute-start.2 = (f32[121,16]{1,0:T(8,128)}, f32[121,16]{1,0:T(8,128)}, u32[]{:S(2)}, u32[]{:S(2)}) collective-permute-start(f32[121,16]{1,0:T(8,128)} %get-tuple-element.16), channel_id=1, source_target_pairs={{16,0},{32,16},{48,32},{64,48},{80,64},{96,80},{112,96},{128,112},... | collective-permute-start | bytes 23240 | tf_op jit(solution)/shard_map/ppermute | solution.py:325
  70.2 6.4 %copy-start.3 = (f32[32,8,128]{2,1,0:T(8,128)S(1)}, f32[32,8,128]{2,1,0:T(8,128)}, u32[]{:S(2)}) copy-start(f32[32,8,128]{2,1,0:T(8,128)} %copy-done.2) | copy-start | bytes 393220
  70.3 10.4 %copy-start.1 = (f32[64,1024]{1,0:T(8,128)S(1)}, f32[64,1024]{1,0:T(8,128)}, u32[]{:S(2)}) copy-start(f32[64,1024]{1,0:T(8,128)} %weight_ref.1) | copy-start | bytes 786436
  70.3 6.3 %collective-permute-start = (f32[1,256,128]{2,1,0:T(8,128)}, f32[1,256,128]{2,1,0:T(8,128)S(1)}, u32[]{:S(2)}, u32[]{:S(2)}) collective-permute-start(f32[1,256,128]{2,1,0:T(8,128)} %bitcast.34), channel_id=1, source_target_pairs={{0,128},{16,144},{32,160},{48,176},{64,192},{80,208},{96,224},{112... | collective-permute-start | bytes 393224 | tf_op jit(solution)/shard_map/ppermute | solution.py:312
